TPU v7x, 32 devices: a whole 2x2x4 slice. The times are simulated.
32 devices in a mesh: groups: 2 (over x), pair: 16 (over z, y, core).
Axes of the slice: x: 2, y: 2, z: 4, core: 2. Of those that a mesh axis runs over, the one named last changes fastest.
Arguments:
- density: bfloat16 [256, 48, 256], P(('groups', 'pair')), parts along dimension 0, may hold values from -6 to 6
- three_index: bfloat16 [256, 32, 128, 256], P(('groups', 'pair')), parts along dimension 0, may hold values from -0.09375 to 0.09375
- live: int32 [256], P(('groups', 'pair')), parts along dimension 0, may hold values from 1 to 32, as said below
- screen: int32 [256, 32], P(('groups', 'pair')), parts along dimension 0, may hold values from 0 to 31
- metric_inverse: float32 [4096, 4096], P('pair'), as said below
Outputs:
- response: bfloat16 [256, 48, 256], P(('groups', 'pair')), parts along dimension 0
- coefficients: float32 [64, 48, 128], P(('groups', 'pair')), parts along dimension 0
There are 2 independent parts, one for each index of `groups`. A program takes and returns all parts, laid end to end along the dimension named above; an argument that names none is the same for every part. Nothing has to cross between parts.
Inputs may be any that keep to these rules, and one draw needn't show every extreme that they name: `live`: at least one block has all 32 slots in use. `metric_inverse`: lower triangular with a positive diagonal.
All inputs are finite; a program needn't handle non-finite values.
Results may differ from a plain program's by a relative error of at most 0.0049.
Values may be sent and summed in bfloat16 or wider, within the bound.
No kernel may reach another device: no remote copies, remote signals or barrier semaphores. Data moves between devices by JAX's collectives and lax.ppermute only.
A program may use at most 128 MiB of HBM per device.

v0:
```python
import jax
import jax.numpy as jnp
from jax import lax
from jax.sharding import PartitionSpec as P


def per_device(density, three_index, live, screen, metric_inverse):
    blocks, slots_count = screen.shape
    aux_blk = three_index.shape[2]
    states = density.shape[1]
    own_blocks = metric_inverse.shape[0] // aux_blk
    total_blocks = metric_inverse.shape[1] // aux_blk
    slots = lax.broadcasted_iota(jnp.int32, screen.shape, 1)
    mask = (slots < live[:, None]).astype(jnp.float32)
    contrib = jnp.einsum("bkrj,bsj->bksr", three_index, density, preferred_element_type=jnp.float32)
    labels = lax.broadcasted_iota(jnp.int32, (blocks * slots_count, total_blocks), 1)
    onehot = (screen.reshape(-1)[:, None] == labels).astype(jnp.float32) * mask.reshape(-1)[:, None]
    partial_gamma = jnp.einsum(
        "na,nsr->asr", onehot, contrib.reshape(-1, states, aux_blk), precision=lax.Precision.HIGHEST
    )
    gamma_full = lax.psum(partial_gamma, "pair")
    metric = metric_inverse.reshape(own_blocks, aux_blk, total_blocks, aux_blk)
    fitted = jnp.einsum("xrqt,qst->xsr", metric, gamma_full, precision=lax.Precision.HIGHEST)
    coefficients = lax.psum_scatter(
        jnp.einsum("xrqt,xsr->qst", metric, fitted, precision=lax.Precision.HIGHEST),
        "pair",
        scatter_dimension=0,
        tiled=True,
    )
    rounded = lax.all_gather(coefficients.astype(jnp.bfloat16), "pair", axis=0, tiled=True)
    picked = rounded[screen] * mask[:, :, None, None].astype(jnp.bfloat16)
    response = jnp.einsum("bkrj,bksr->bsj", three_index, picked, preferred_element_type=jnp.float32)
    return (response.astype(jnp.bfloat16), coefficients)


def solution(mesh):
    placed = (
        P(("groups", "pair"), None, None),
        P(("groups", "pair"), None, None, None),
        P(("groups", "pair")),
        P(("groups", "pair"), None),
        P("pair", None),
    )
    return jax.shard_map(
        per_device,
        mesh=mesh,
        in_specs=placed,
        out_specs=(P(("groups", "pair"), None, None), P(("groups", "pair"), None, None)),
        check_vma=False,
    )
```

profile of v0, /device:TPU:0, one launch (start us, length us, event | category | flops | bytes accessed | tf_op | source)
XLA Modules:
  0.0 237.5 jit_solution(15537850468128110723)
XLA Ops:
  7.2 0.0 copy-start
  7.2 0.0 all-reduce.2.cloned.1.call-start
  7.2 0.8 fusion.30
  8.0 0.1 reshape.51
  8.1 0.8 eq.10
  8.8 0.0 copy-done
  8.8 13.4 %fusion.22 = f32[8,48,32,128]{3,1,2,0:T(8,128)} fusion(bf16[8,32,128,256]{3,2,1,0:T(8,128)(2,1)} %param.6, bf16[8,48,256]{2,1,0:T(8,128)(2,1)S(1)} %copy-done), kind=kOutput, calls=%fused_computation.15 | convolution fusion | flops 805306368 | bytes 23265280 | tf_op jit(solution)/shard_map/bkrj,bsj->bksr/dot_general | solution.py:15
  22.2 7.7 %fusion = f32[32,48,128]{2,0,1:T(8,128)S(1)} fusion(f32[256,48,128]{2,1,0:T(8,128)} %bitcast.38, f32[256]{0:T(256)S(1)} %reshape.51, s32[256]{0:T(256)S(1)} %eq.10), kind=kOutput, calls=%fused_computation.1 | convolution fusion | flops 603996160 | bytes 7079936 | tf_op jit(solution)/shard_map/na,nsr->asr/dot_general | solution.py:18
  30.0 1.4 copy.11
  31.3 0.0 all-reduce.2.cloned.1.call-update
  31.3 0.2 reduce-scatter.2.cloned.1.call-start
  31.6 4.9 %copy.16 = f32[32,8,32,128]{3,2,1,0:T(8,128)} copy(f32[32,8,32,128]{3,1,2,0:T(8,128)} %bitcast.42) | data formatting | bytes 8388608
  36.4 89.8 %all-reduce.2.cloned.1.call-done = f32[32,48,128]{2,1,0:T(8,128)} async-done(((f32[32,48,128]{2,1,0:T(8,128)}), f32[32,48,128]{2,1,0:T(8,128)}) %all-reduce.2.cloned.1.call-update) | async-done | bytes 786448 | tf_op jit(solution)/shard_map/psum | solution.py:21
  126.2 0.0 copy-start.1
  126.2 0.0 copy-start.2
  126.2 8.5 %fusion.18 = f32[2,48,128,1]{2,1,0,3:T(8,128)S(1)} fusion(f32[2,128,32,128]{3,2,1,0:T(8,128)} %bitcast.39, f32[32,48,128]{2,1,0:T(8,128)} %all-reduce.2.cloned.1.call-done), kind=kOutput, calls=%fused_computation.13 | convolution fusion | flops 603979776 | bytes 5029888 | tf_op jit(solution)/shard_map/xrqt,qst->xsr/dot_general | solution.py:23
  134.8 0.0 copy-done.1
  134.8 5.8 %fusion.9 = f32[32,48,128]{2,1,0:T(8,128)} fusion(f32[2,48,128,1]{2,1,0,3:T(8,128)S(1)} %fusion.18, f32[2,128,32,128]{3,2,1,0:T(8,128)S(1)} %bitcast.40), kind=kOutput, calls=%fused_computation.10 | convolution fusion | flops 603979776 | bytes 5029888 | tf_op jit(solution)/shard_map/xrqt,xsr->qst/dot_general | solution.py:25
  140.5 0.0 reduce-scatter.2.cloned.1.call-update
  140.6 0.0 copy-done.2
  140.6 0.1 reshape.54
  140.7 55.6 %reduce-scatter.2.cloned.1.call-done = f32[2,48,128]{2,1,0:T(8,128)} async-done(((f32[32,48,128]{2,1,0:T(8,128)}), f32[2,48,128]{2,1,0:T(8,128)}) %reduce-scatter.2.cloned.1.call-update) | async-done | bytes 49168 | tf_op jit(solution)/shard_map/reduce_scatter | solution.py:24
  196.2 0.8 convert_element_type.33
  197.0 20.5 %all_gather.3 = bf16[32,48,128]{2,1,0:T(8,128)(2,1)S(1)} all-gather(bf16[2,48,128]{2,1,0:T(8,128)(2,1)S(1)} %convert_element_type.33), channel_id=1, replica_groups=mesh['groups'=2,'pair'=16] {'pair'}, dimensions={0}, use_global_device_ids=true | all-gather | bytes 417792 | tf_op jit(solution)/shard_map/all_gather | solution.py:30
  217.5 2.6 %gather_fusion = bf16[256,48,128]{2,1,0:T(8,128)(2,1)} fusion(bf16[32,48,128]{2,1,0:T(8,128)(2,1)S(1)} %all_gather.3, s32[1024]{0:T(1024)S(1)} %pad_clamp_fusion), kind=kCustom, calls=%fused_computation | custom fusion | bytes 6292480 | tf_op jit(solution)/shard_map/gather | solution.py:31
  220.2 10.5 %fusion.15 = bf16[8,48,256]{2,1,0:T(8,128)(2,1)} fusion(bf16[8,32,128,256]{3,2,1,0:T(8,128)(2,1)} %param.6, bf16[8,32,48,128]{3,2,1,0:T(8,128)(2,1)} %bitcast.41, bf16[8,32]{1,0:T(8,128)(2,1)S(1)} %get-tuple-element.2), kind=kOutput, calls=%fused_computation.12 | convolution fusion | flops 806977536 | bytes 20120064 | tf_op jit(solution)/shard_map/bkrj,bksr->bsj/dot_general | solution.py:32
  (2 shorter events, 0.0 us)
Async XLA Ops:
  7.2 1.7 copy-start
  7.2 119.0 %all-reduce.2.cloned.1.call-start = ((), (), s32[]{:S(2)}) async-start(), calls=%async_computation.1 | async-start | bytes 1572864 | tf_op jit(solution)/shard_map/psum | solution.py:21
  31.3 164.9 %reduce-scatter.2.cloned.1.call-start = ((), (), s32[]{:S(2)}) async-start(), calls=%async_computation.2 | async-start | bytes 835584 | tf_op jit(solution)/shard_map/reduce_scatter | solution.py:24
  126.2 8.6 %copy-start.1 = (f32[32,8,32,128]{3,2,1,0:T(8,128)S(1)}, f32[32,8,32,128]{3,2,1,0:T(8,128)}, u32[]{:S(2)}) copy-start(f32[32,8,32,128]{3,2,1,0:T(8,128)} %copy.16) | copy-start | bytes 12582916
  126.2 14.3 %copy-start.2 = (s32[8,32]{1,0:T(8,128)S(1)}, s32[8,32]{1,0:T(8,128)}, u32[]{:S(2)}) copy-start(s32[8,32]{1,0:T(8,128)} %param.8) | copy-start | bytes 3076
Sparse Core Ops, SparseCore 0:
  31.5 94.7 all-reduce.1
  140.7 55.5 reduce-scatter.1
where the time goes:
time: 238 us; the launch traced here: 237 us
  waiting for transfers between devices  145 us (61%)
  matrix products  45.9 us (19%)
  blocking collectives  20.5 us (9%)
  between operations  14.1 us (6%)
  local copies, waits for them, and re-layouts  9.79 us (4%)
    psum x1, waiting for transfers between devices, per_device(): gamma_full = lax.psum(partial_gamma, 'pair')  89.8 us
    reduce_scatter x1, waiting for transfers between devices, per_device(): lax.psum_scatter(jnp.einsum('xrqt,xsr->qst', metric, fitted, precision=la...  55.6 us
    all_gather x1, blocking collectives, per_device(): lax.all_gather(coefficients.astype(jnp.bfloat16), 'pair', axis=0, tiled=T...  20.5 us
    dot_general x1, matrix products, per_device(): jnp.einsum('bkrj,bsj->bksr', three_index, density, preferred_element_type...  13.4 us
    dot_general x1, matrix products, per_device(): jnp.einsum('bkrj,bksr->bsj', three_index, picked, preferred_element_type=...  10.5 us
    dot_general x1, matrix products, per_device(): jnp.einsum('xrqt,qst->xsr', metric, gamma_full, precision=lax.Precision.H...  8.54 us
    dot_general x1, matrix products, per_device(): jnp.einsum('na,nsr->asr', onehot, contrib.reshape(-1, states, aux_blk), p...  7.71 us
    dot_general x1, matrix products, per_device(): jnp.einsum('xrqt,xsr->qst', metric, fitted, precision=lax.Precision.HIGHEST)  5.76 us
  transfers between devices with their start and end apart: 2, of which 2 were waited for; matrix products, arithmetic and copies ran while one was open for 2% of the time, Pallas kernels for 0%

commit v1 on v0

v1 whole, which is shorter than its diff:
```python
import functools

import jax
import jax.numpy as jnp
from jax import lax
from jax.experimental import pallas as pl
from jax.experimental.pallas import tpu as pltpu
from jax.sharding import PartitionSpec as P

F32 = jnp.float32
BF16 = jnp.bfloat16
NT = (((1,), (1,)), ((), ()))
NN = (((1,), (0,)), ((), ()))
PAIRS = 8
MIB = 2**20


def row_of(a, own, half, me):
    side = (a // own) % 2
    return jnp.where(side == me, 0, half) + (a // (2 * own)) * own + a % own


def fetch(live_h, screen_h, table_h, live, screen, slots, table, small_sem, table_sem):
    blocks, per_block = screen.shape
    aux = table.shape[0] // (blocks * per_block)
    first = pltpu.make_async_copy(live_h, live, small_sem.at[0])
    second = pltpu.make_async_copy(screen_h, screen, small_sem.at[1])
    first.start()
    second.start()
    first.wait()
    for b in range(blocks):
        block_copy(table_h, table, table_sem, live, b, per_block * aux, aux).start()

    def block(b, total):
        pairs = (live[b] + 1) // 2

        def one(p, _):
            slots[total + p] = b * per_block + 2 * p
            return 0

        lax.fori_loop(0, pairs, one, 0)
        return total + pairs

    total = lax.fori_loop(0, blocks, block, 0)
    for p in range(PAIRS):
        slots[total + p] = 0
    second.wait()
    return total


def block_copy(table_h, table, table_sem, live, b, block_rows, aux):
    rows = pl.multiple_of((live[b] + 1) // 2 * 2 * aux, 2 * aux)
    part = pl.ds(pl.multiple_of(b * block_rows, 2 * aux), rows)
    return pltpu.make_async_copy(table_h.at[part], table.at[part], table_sem.at[b])


def pair_at(i, slots, live, screen, total, dead, own, half, me):
    per_block = screen.shape[1]
    slot = slots[i]
    b, t = slot // per_block, slot % per_block
    rows = [row_of(screen[b, t + k], own, half, me) for k in (0, 1)]
    rows = [jnp.where((i < total) & (t + k < live[b]), rows[k], dead) for k in (0, 1)]
    return slot, b, t, rows


def gamma_kernel(own, axis, live_h, screen_h, density_h, table_h, keep, send, live, screen, slots, density, table, acc, small_sem, table_sem):
    blocks, per_block = screen.shape
    half, states, aux = keep.shape
    me = lax.axis_index(axis) % 2
    third = pltpu.make_async_copy(density_h, density, small_sem.at[2])
    third.start()
    total = fetch(live_h, screen_h, table_h, live, screen, slots, table, small_sem, table_sem)
    acc[...] = jnp.zeros_like(acc)
    third.wait()

    def chunk(c, _):
        results = []
        for p in range(PAIRS):
            i = c * PAIRS + p
            slot, b, t, rows = pair_at(i, slots, live, screen, total, 2 * half, own, half, me)

            @pl.when((t == 0) & (i < total))
            def _():
                block_copy(table_h, table, table_sem, live, b, per_block * aux, aux).wait()

            results.append((slot, b, rows))
        products = []
        for slot, b, rows in results:
            tile = table[pl.ds(pl.multiple_of(slot * aux, 2 * aux), 2 * aux), :]
            products.append(lax.dot_general(density[b], tile, NT, preferred_element_type=F32))
        for (slot, b, rows), product in zip(results, products):
            for k in (0, 1):
                acc[rows[k]] = acc[rows[k]] + product[:, k * aux : (k + 1) * aux]
        return 0

    lax.fori_loop(0, (total + PAIRS - 1) // PAIRS, chunk, 0)
    keep[...] = acc[0:half]
    send[...] = acc[half : 2 * half].astype(send.dtype)


def response_kernel(own, axis, live_h, screen_h, table_h, coef_own, coef_other, out, live, screen, slots, table, coef, acc, small_sem, table_sem):
    blocks, per_block = screen.shape
    half, states, aux = coef_own.shape
    me = lax.axis_index(axis) % 2
    total = fetch(live_h, screen_h, table_h, live, screen, slots, table, small_sem, table_sem)
    acc[...] = jnp.zeros_like(acc)
    coef[0:half] = coef_own[...]
    coef[half : 2 * half] = coef_other[...]
    coef[2 * half] = jnp.zeros((states, aux), BF16)

    def chunk(c, _):
        results = []
        for p in range(PAIRS):
            i = c * PAIRS + p
            slot, b, t, rows = pair_at(i, slots, live, screen, total, 2 * half, own, half, me)

            @pl.when((t == 0) & (i < total))
            def _():
                block_copy(table_h, table, table_sem, live, b, per_block * aux, aux).wait()

            results.append((slot, b, rows))
        products = []
        for slot, b, rows in results:
            tile = table[pl.ds(pl.multiple_of(slot * aux, 2 * aux), 2 * aux), :]
            picked = jnp.concatenate([coef[rows[0]], coef[rows[1]]], axis=1)
            products.append(lax.dot_general(picked, tile, NN, preferred_element_type=F32))
        for (slot, b, rows), product in zip(results, products):
            acc[b] = acc[b] + product
        return 0

    lax.fori_loop(0, (total + PAIRS - 1) // PAIRS, chunk, 0)
    out[...] = acc[...].astype(out.dtype)


def metric_kernel(own, axis, gamma_own, gamma_other, metric, keep, send, high, low):
    half, states, aux = keep.shape
    rows = metric.shape[0]
    width = own * aux
    me = lax.axis_index(axis) % 2
    sides = [(gamma_own, keep, me), (gamma_other, send, 1 - me)]
    fitted = jnp.zeros((states, rows), F32)
    for chip in range(half // own):
        for gamma, _, side in sides:
            part = pl.ds(pl.multiple_of((chip * 2 + side) * width, width), width)
            whole = metric[:, part]
            h = whole.astype(BF16)
            l = (whole - h.astype(F32)).astype(BF16)
            high[:, part] = h
            low[:, part] = l
            g = jnp.concatenate([gamma[chip * own + k] for k in range(own)], axis=1)
            fitted += lax.dot_general(g, h, NT, preferred_element_type=F32)
            fitted += lax.dot_general(g, l, NT, preferred_element_type=F32)
    fitted_high = fitted.astype(BF16)
    fitted_low = (fitted - fitted_high.astype(F32)).astype(BF16)
    for chip in range(half // own):
        for _, out, side in sides:
            part = pl.ds(pl.multiple_of((chip * 2 + side) * width, width), width)
            h, l = high[:, part], low[:, part]
            c = lax.dot_general(fitted_high, h, NN, preferred_element_type=F32)
            c += lax.dot_general(fitted_high, l, NN, preferred_element_type=F32)
            c += lax.dot_general(fitted_low, h, NN, preferred_element_type=F32)
            for k in range(own):
                out[chip * own + k] = c[:, k * aux : (k + 1) * aux].astype(out.dtype)


def exchange(x, axis, devices, bit):
    return lax.ppermute(x, axis, [(j, j ^ bit) for j in range(devices)])


def summed(keep, send, axis, devices):
    total = keep + exchange(send, axis, devices, 1).astype(F32)
    bit = 2
    while bit < devices:
        total = total + exchange(total.astype(BF16), axis, devices, bit).astype(F32)
        bit *= 2
    return total


def per_device(devices, density, three_index, live, screen, metric_inverse):
    axis = "pair"
    blocks, per_block = screen.shape
    states = density.shape[1]
    aux, pairs = three_index.shape[2:]
    own = metric_inverse.shape[0] // aux
    half = metric_inverse.shape[1] // aux // 2
    table = three_index.reshape(blocks * per_block * aux, pairs)
    hbm = pl.BlockSpec(memory_space=pltpu.HBM)
    vmem = pl.BlockSpec(memory_space=pltpu.VMEM)
    lists = [
        pltpu.SMEM((blocks,), jnp.int32),
        pltpu.SMEM((blocks, per_block), jnp.int32),
        pltpu.SMEM((blocks * per_block // 2 + PAIRS,), jnp.int32),
    ]
    sems = [pltpu.SemaphoreType.DMA((3,)), pltpu.SemaphoreType.DMA((blocks,))]
    halves = (jax.ShapeDtypeStruct((half, states, aux), F32), jax.ShapeDtypeStruct((half, states, aux), F32))
    flops = 2 * blocks * per_block * aux * pairs * states

    keep, send = pl.pallas_call(
        functools.partial(gamma_kernel, own, axis),
        out_shape=halves,
        in_specs=[hbm] * 4,
        out_specs=(vmem, vmem),
        scratch_shapes=lists
        + [pltpu.VMEM(density.shape, BF16), pltpu.VMEM(table.shape, BF16), pltpu.VMEM((2 * half + 1, states, aux), F32)]
        + sems,
        compiler_params=pltpu.CompilerParams(vmem_limit_bytes=40 * MIB),
        cost_estimate=pl.CostEstimate(flops=flops, bytes_accessed=table.size * 2, transcendentals=0),
        name="gamma",
    )(live, screen, density, table)
    gamma = summed(keep, send, axis, devices).astype(BF16)
    gamma_other = exchange(gamma, axis, devices, 1)

    keep, send = pl.pallas_call(
        functools.partial(metric_kernel, own, axis),
        out_shape=halves,
        in_specs=[vmem] * 3,
        out_specs=(vmem, vmem),
        scratch_shapes=[pltpu.VMEM(metric_inverse.shape, BF16)] * 2,
        compiler_params=pltpu.CompilerParams(vmem_limit_bytes=24 * MIB),
        cost_estimate=pl.CostEstimate(flops=10 * metric_inverse.size * states, bytes_accessed=metric_inverse.size * 4, transcendentals=0),
        name="metric",
    )(gamma, gamma_other, metric_inverse)
    total = summed(keep, send, axis, devices)
    mine = (lax.axis_index(axis) // 2) * own
    coefficients = lax.dynamic_slice_in_dim(total, mine, own, axis=0)
    rounded = total.astype(BF16)
    rounded_other = exchange(rounded, axis, devices, 1)

    response = pl.pallas_call(
        functools.partial(response_kernel, own, axis),
        out_shape=jax.ShapeDtypeStruct(density.shape, BF16),
        in_specs=[hbm] * 3 + [vmem] * 2,
        out_specs=vmem,
        scratch_shapes=lists
        + [pltpu.VMEM(table.shape, BF16), pltpu.VMEM((2 * half + 1, states, aux), BF16), pltpu.VMEM(density.shape, F32)]
        + sems,
        compiler_params=pltpu.CompilerParams(vmem_limit_bytes=40 * MIB),
        cost_estimate=pl.CostEstimate(flops=flops, bytes_accessed=table.size * 2, transcendentals=0),
        name="response",
    )(live, screen, table, rounded, rounded_other)
    return (response, coefficients)


def solution(mesh):
    devices = mesh.shape["pair"]
    placed = (
        P(("groups", "pair"), None, None),
        P(("groups", "pair"), None, None, None),
        P(("groups", "pair")),
        P(("groups", "pair"), None),
        P("pair", None),
    )
    return jax.shard_map(
        functools.partial(per_device, devices),
        mesh=mesh,
        in_specs=placed,
        out_specs=(P(("groups", "pair"), None, None), P(("groups", "pair"), None, None)),
        check_vma=False,
    )
```

time: 238 us -> 83.9 us (0.35)
  the two profiles are of different devices: /device:TPU:0 before, /device:TPU:3 now
where the time goes in v1:
time: 83.9 us; the launch traced here: 82.7 us
  waiting for transfers between devices  46.2 us (55%)
  Pallas kernels  22.7 us (27%)
  starting transfers between devices  9.19 us (11%)
  local copies, waits for them, and re-layouts  3.31 us (4%)
    ppermute x10, waiting for transfers between devices, exchange(): return lax.ppermute(x, axis, [(j, j ^ bit) for j in range(devices)])  46.2 us
    pallas_call x1, Pallas kernels, per_device(): pl.pallas_call(functools.partial(gamma_kernel, own, axis), out_shape=halv...  9.7 us
    ppermute x10, starting transfers between devices, exchange(): return lax.ppermute(x, axis, [(j, j ^ bit) for j in range(devices)])  9.19 us
    pallas_call x1, Pallas kernels, per_device(): pl.pallas_call(functools.partial(response_kernel, own, axis), out_shape=j...  8.93 us
    pallas_call x1, Pallas kernels, per_device(): pl.pallas_call(functools.partial(metric_kernel, own, axis), out_shape=hal...  4.04 us
    unnamed x12, local copies, waits for them, and re-layouts  2.69 us
  transfers between devices with their start and end apart: 10, of which 10 were waited for; matrix products, arithmetic and copies ran while one was open for 1% of the time, Pallas kernels for 0%

profile of v1, /device:TPU:3, one launch (start us, length us, event | category | flops | bytes accessed | tf_op | source)
XLA Modules:
  0.0 82.7 jit_solution(2498041686969833677)
XLA Ops:
  0.6 0.0 copy-start
  0.6 0.0 copy-start.1
  0.7 1.1 %copy-done.1 = bf16[8,48,256]{2,1,0:T(8,128)(2,1)S(1)} copy-done((bf16[8,48,256]{2,1,0:T(8,128)(2,1)S(1)}, bf16[8,48,256]{2,1,0:T(8,128)(2,1)}, u32[]{:S(2)}) %copy-start.1) | copy-done | bytes 196632
  1.7 0.0 copy-start.2
  1.7 1.0 %copy-done.2 = s32[8,32]{1,0:T(8,128)S(1)} copy-done((s32[8,32]{1,0:T(8,128)S(1)}, s32[8,32]{1,0:T(8,128)}, u32[]{:S(2)}) %copy-start.2) | copy-done | bytes 1048
  2.7 0.0 copy-start.4
  2.7 0.7 copy-done.4
  3.3 0.0 copy-start.3
  3.3 0.0 copy-start.5
  3.3 9.7 %gamma.1 = (f32[16,48,128]{2,1,0:T(8,128)S(1)}, f32[16,48,128]{2,1,0:T(8,128)S(1)}) custom-call(s32[8]{0:T(128)S(1)} %copy-done.4, s32[8,32]{1,0:T(8,128)S(1)} %copy-done.2, bf16[8,48,256]{2,1,0:T(8,128)(2,1)S(1)} %copy-done.1, bf16[32768,256]{1,0:T(8,128)(2,1)} %bitcast.1), custom_call_target="tpu_custom_call" | custom-call | flops 805306368 | bytes 16777216 | tf_op jit(solution)/shard_map/gamma/pallas_call | solution.py:198
  13.0 0.1 collective-permute-start
  13.1 1.7 %collective-permute-done = f32[16,48,128]{2,1,0:T(8,128)S(1)} collective-permute-done((f32[16,48,128]{2,1,0:T(8,128)S(1)}, f32[16,48,128]{2,1,0:T(8,128)S(1)}, u32[]{:S(2)}, u32[]{:S(2)}) %collective-permute-start) | collective-permute-done | bytes 393248 | tf_op jit(solution)/shard_map/ppermute | solution.py:167
  14.8 0.1 fusion.6
  14.9 0.1 collective-permute-start.1
  15.0 6.3 %collective-permute-done.1 = bf16[16,48,128]{2,1,0:T(8,128)(2,1)S(1)} collective-permute-done((bf16[16,48,128]{2,1,0:T(8,128)(2,1)S(1)}, bf16[16,48,128]{2,1,0:T(8,128)(2,1)S(1)}, u32[]{:S(2)}, u32[]{:S(2)}) %collective-permute-start.1) | collective-permute-done | bytes 196640 | tf_op jit(solution)/shard_map/ppermute | solution.py:167
  21.3 0.1 fusion
  21.4 3.3 %collective-permute-start.2 = (bf16[16,48,128]{2,1,0:T(8,128)(2,1)S(1)}, bf16[16,48,128]{2,1,0:T(8,128)(2,1)S(1)}, u32[]{:S(2)}, u32[]{:S(2)}) collective-permute-start(bf16[16,48,128]{2,1,0:T(8,128)(2,1)S(1)} %fusion), channel_id=1, source_target_pairs={{0,4},{1,5},{2,6},{3,7},{4,0},{5,1},{6,2},{7,3},{8,12},{9,13},{10,... | collective-permute-start | bytes 589832 | tf_op jit(solution)/shard_map/ppermute | solution.py:167
  24.7 4.0 %collective-permute-done.2 = bf16[16,48,128]{2,1,0:T(8,128)(2,1)S(1)} collective-permute-done((bf16[16,48,128]{2,1,0:T(8,128)(2,1)S(1)}, bf16[16,48,128]{2,1,0:T(8,128)(2,1)S(1)}, u32[]{:S(2)}, u32[]{:S(2)}) %collective-permute-start.2) | collective-permute-done | bytes 196640 | tf_op jit(solution)/shard_map/ppermute | solution.py:167
  28.7 0.1 fusion.2
  28.8 1.8 %collective-permute-start.3 = (bf16[16,48,128]{2,1,0:T(8,128)(2,1)S(1)}, bf16[16,48,128]{2,1,0:T(8,128)(2,1)S(1)}, u32[]{:S(2)}, u32[]{:S(2)}) collective-permute-start(bf16[16,48,128]{2,1,0:T(8,128)(2,1)S(1)} %fusion.2), channel_id=1, source_target_pairs={{0,8},{1,9},{2,10},{3,11},{4,12},{5,13},{6,14},{7,15},{8,0},{9,1},... | collective-permute-start | bytes 589832 | tf_op jit(solution)/shard_map/ppermute | solution.py:167
  30.6 9.3 %collective-permute-done.3 = bf16[16,48,128]{2,1,0:T(8,128)(2,1)S(1)} collective-permute-done((bf16[16,48,128]{2,1,0:T(8,128)(2,1)S(1)}, bf16[16,48,128]{2,1,0:T(8,128)(2,1)S(1)}, u32[]{:S(2)}, u32[]{:S(2)}) %collective-permute-start.3) | collective-permute-done | bytes 196640 | tf_op jit(solution)/shard_map/ppermute | solution.py:167
  39.9 0.1 add_convert_fusion.gamma_own
  40.0 1.5 %collective-permute-start.4 = (bf16[16,48,128]{2,1,0:T(8,128)(2,1)S(1)}, bf16[16,48,128]{2,1,0:T(8,128)(2,1)S(1)}, u32[]{:S(2)}, u32[]{:S(2)}) collective-permute-start(bf16[16,48,128]{2,1,0:T(8,128)(2,1)S(1)} %add_convert_fusion.gamma_own), channel_id=1, source_target_pairs={{0,1},{1,0},{2,3},{3,2},{4,5},{5,4},{6,7},{7,6},{8,9},{9,8},{10,11... | collective-permute-start | bytes 589832 | tf_op jit(solution)/shard_map/ppermute | solution.py:167
  41.5 1.1 %collective-permute-done.4.gamma_other = bf16[16,48,128]{2,1,0:T(8,128)(2,1)S(1)} collective-permute-done((bf16[16,48,128]{2,1,0:T(8,128)(2,1)S(1)}, bf16[16,48,128]{2,1,0:T(8,128)(2,1)S(1)}, u32[]{:S(2)}, u32[]{:S(2)}) %collective-permute-start.4) | collective-permute-done | bytes 196640 | tf_op jit(solution)/shard_map/ppermute | solution.py:167
  42.6 0.0 copy-done
  42.6 4.0 %metric.2 = (f32[16,48,128]{2,1,0:T(8,128)S(1)}, f32[16,48,128]{2,1,0:T(8,128)S(1)}) custom-call(bf16[16,48,128]{2,1,0:T(8,128)(2,1)S(1)} %add_convert_fusion.gamma_own, bf16[16,48,128]{2,1,0:T(8,128)(2,1)S(1)} %collective-permute-done.4.gamma_other, f32[256,4096]{1,0:T(8,128)S(1)} %copy-done), custom_call_target="tpu_custom_call" | custom-call | flops 503316480 | bytes 4194304 | tf_op jit(solution)/shard_map/metric/pallas_call | solution.py:213
  46.6 0.4 collective-permute-start.5
  47.0 1.4 %collective-permute-done.5 = f32[16,48,128]{2,1,0:T(8,128)S(1)} collective-permute-done((f32[16,48,128]{2,1,0:T(8,128)S(1)}, f32[16,48,128]{2,1,0:T(8,128)S(1)}, u32[]{:S(2)}, u32[]{:S(2)}) %collective-permute-start.5) | collective-permute-done | bytes 393248 | tf_op jit(solution)/shard_map/ppermute | solution.py:167
  48.3 0.1 fusion.5
  48.4 0.8 collective-permute-start.6
  49.1 5.4 %collective-permute-done.6 = bf16[16,48,128]{2,1,0:T(8,128)(2,1)S(1)} collective-permute-done((bf16[16,48,128]{2,1,0:T(8,128)(2,1)S(1)}, bf16[16,48,128]{2,1,0:T(8,128)(2,1)S(1)}, u32[]{:S(2)}, u32[]{:S(2)}) %collective-permute-start.6) | collective-permute-done | bytes 196640 | tf_op jit(solution)/shard_map/ppermute | solution.py:167
  54.6 0.1 fusion.1
  54.6 0.1 collective-permute-start.7
  54.7 5.2 %collective-permute-done.7 = bf16[16,48,128]{2,1,0:T(8,128)(2,1)S(1)} collective-permute-done((bf16[16,48,128]{2,1,0:T(8,128)(2,1)S(1)}, bf16[16,48,128]{2,1,0:T(8,128)(2,1)S(1)}, u32[]{:S(2)}, u32[]{:S(2)}) %collective-permute-start.7) | collective-permute-done | bytes 196640 | tf_op jit(solution)/shard_map/ppermute | solution.py:167
  59.9 0.1 fusion.3
  60.0 0.6 collective-permute-start.8
  60.6 11.3 %collective-permute-done.8 = bf16[16,48,128]{2,1,0:T(8,128)(2,1)S(1)} collective-permute-done((bf16[16,48,128]{2,1,0:T(8,128)(2,1)S(1)}, bf16[16,48,128]{2,1,0:T(8,128)(2,1)S(1)}, u32[]{:S(2)}, u32[]{:S(2)}) %collective-permute-start.8) | collective-permute-done | bytes 196640 | tf_op jit(solution)/shard_map/ppermute | solution.py:167
  71.9 0.1 fusion.4
  72.0 0.6 collective-permute-start.9
  72.7 0.6 constant_dynamic-slice_fusion
  73.3 0.4 collective-permute-done.9.coef_other
  73.7 0.0 copy-done.3
  73.7 0.0 copy-done.5
  73.7 8.9 %response.1 = bf16[8,48,256]{2,1,0:T(8,128)(2,1)} custom-call(s32[8]{0:T(128)S(1)} %copy-done.5, s32[8,32]{1,0:T(8,128)S(1)} %copy-done.3, bf16[32768,256]{1,0:T(8,128)(2,1)} %bitcast.2, bf16[16,48,128]{2,1,0:T(8,128)(2,1)S(1)} %get-tuple-element.10.coef_own, bf16[16,48,128]{2,1,0:T(8,128)(2,1)S(1)} %collective-permute-done.9.coef_other), custom_call_target="tpu_custom_call" | custom-call | flops 805306368 | bytes 16777216 | tf_op jit(solution)/shard_map/response/pallas_call | solution.py:229
Async XLA Ops:
  0.6 41.9 %copy-start = (f32[256,4096]{1,0:T(8,128)S(1)}, f32[256,4096]{1,0:T(8,128)}, u32[]{:S(2)}) copy-start(f32[256,4096]{1,0:T(8,128)} %metric.3) | copy-start | bytes 12582916
  0.6 1.1 %copy-start.1 = (bf16[8,48,256]{2,1,0:T(8,128)(2,1)S(1)}, bf16[8,48,256]{2,1,0:T(8,128)(2,1)}, u32[]{:S(2)}) copy-start(bf16[8,48,256]{2,1,0:T(8,128)(2,1)} %density_h.1) | copy-start | bytes 589828
  1.7 1.0 %copy-start.2 = (s32[8,32]{1,0:T(8,128)S(1)}, s32[8,32]{1,0:T(8,128)}, u32[]{:S(2)}) copy-start(s32[8,32]{1,0:T(8,128)} %screen_h.3) | copy-start | bytes 3076
  2.7 0.7 copy-start.4
  3.3 70.4 %copy-start.3 = (s32[8,32]{1,0:T(8,128)S(1)}, s32[8,32]{1,0:T(8,128)}, u32[]{:S(2)}) copy-start(s32[8,32]{1,0:T(8,128)} %screen_h.3) | copy-start | bytes 3076
  3.3 70.4 %copy-start.5 = (s32[8]{0:T(128)S(1)}, s32[8]{0:T(128)}, u32[]{:S(2)}) copy-start(s32[8]{0:T(128)} %live_h.3) | copy-start | bytes 100
  13.0 1.8 %collective-permute-start = (f32[16,48,128]{2,1,0:T(8,128)S(1)}, f32[16,48,128]{2,1,0:T(8,128)S(1)}, u32[]{:S(2)}, u32[]{:S(2)}) collective-permute-start(f32[16,48,128]{2,1,0:T(8,128)S(1)} %get-tuple-element.7), channel_id=1, source_target_pairs={{0,1},{1,0},{2,3},{3,2},{4,5},{5,4},{6,7},{7,6},{8,9},{9,8},{10,11... | collective-permute-start | bytes 1179656 | tf_op jit(solution)/shard_map/ppermute | solution.py:167
  14.9 6.4 %collective-permute-start.1 = (bf16[16,48,128]{2,1,0:T(8,128)(2,1)S(1)}, bf16[16,48,128]{2,1,0:T(8,128)(2,1)S(1)}, u32[]{:S(2)}, u32[]{:S(2)}) collective-permute-start(bf16[16,48,128]{2,1,0:T(8,128)(2,1)S(1)} %get-tuple-element.14), channel_id=1, source_target_pairs={{0,2},{1,3},{2,0},{3,1},{4,6},{5,7},{6,4},{7,5},{8,10},{9,11},{10,... | collective-permute-start | bytes 589832 | tf_op jit(solution)/shard_map/ppermute | solution.py:167
  21.4 7.4 %collective-permute-start.2 = (bf16[16,48,128]{2,1,0:T(8,128)(2,1)S(1)}, bf16[16,48,128]{2,1,0:T(8,128)(2,1)S(1)}, u32[]{:S(2)}, u32[]{:S(2)}) collective-permute-start(bf16[16,48,128]{2,1,0:T(8,128)(2,1)S(1)} %fusion), channel_id=1, source_target_pairs={{0,4},{1,5},{2,6},{3,7},{4,0},{5,1},{6,2},{7,3},{8,12},{9,13},{10,... | collective-permute-start | bytes 589832 | tf_op jit(solution)/shard_map/ppermute | solution.py:167
  28.8 11.1 %collective-permute-start.3 = (bf16[16,48,128]{2,1,0:T(8,128)(2,1)S(1)}, bf16[16,48,128]{2,1,0:T(8,128)(2,1)S(1)}, u32[]{:S(2)}, u32[]{:S(2)}) collective-permute-start(bf16[16,48,128]{2,1,0:T(8,128)(2,1)S(1)} %fusion.2), channel_id=1, source_target_pairs={{0,8},{1,9},{2,10},{3,11},{4,12},{5,13},{6,14},{7,15},{8,0},{9,1},... | collective-permute-start | bytes 589832 | tf_op jit(solution)/shard_map/ppermute | solution.py:167
  40.0 2.6 %collective-permute-start.4 = (bf16[16,48,128]{2,1,0:T(8,128)(2,1)S(1)}, bf16[16,48,128]{2,1,0:T(8,128)(2,1)S(1)}, u32[]{:S(2)}, u32[]{:S(2)}) collective-permute-start(bf16[16,48,128]{2,1,0:T(8,128)(2,1)S(1)} %add_convert_fusion.gamma_own), channel_id=1, source_target_pairs={{0,1},{1,0},{2,3},{3,2},{4,5},{5,4},{6,7},{7,6},{8,9},{9,8},{10,11... | collective-permute-start | bytes 589832 | tf_op jit(solution)/shard_map/ppermute | solution.py:167
  46.6 1.7 %collective-permute-start.5 = (f32[16,48,128]{2,1,0:T(8,128)S(1)}, f32[16,48,128]{2,1,0:T(8,128)S(1)}, u32[]{:S(2)}, u32[]{:S(2)}) collective-permute-start(f32[16,48,128]{2,1,0:T(8,128)S(1)} %get-tuple-element.9), channel_id=1, source_target_pairs={{0,1},{1,0},{2,3},{3,2},{4,5},{5,4},{6,7},{7,6},{8,9},{9,8},{10,11... | collective-permute-start | bytes 1179656 | tf_op jit(solution)/shard_map/ppermute | solution.py:167
  48.4 6.2 %collective-permute-start.6 = (bf16[16,48,128]{2,1,0:T(8,128)(2,1)S(1)}, bf16[16,48,128]{2,1,0:T(8,128)(2,1)S(1)}, u32[]{:S(2)}, u32[]{:S(2)}) collective-permute-start(bf16[16,48,128]{2,1,0:T(8,128)(2,1)S(1)} %get-tuple-element.12), channel_id=1, source_target_pairs={{0,2},{1,3},{2,0},{3,1},{4,6},{5,7},{6,4},{7,5},{8,10},{9,11},{10,... | collective-permute-start | bytes 589832 | tf_op jit(solution)/shard_map/ppermute | solution.py:167
  54.6 5.3 %collective-permute-start.7 = (bf16[16,48,128]{2,1,0:T(8,128)(2,1)S(1)}, bf16[16,48,128]{2,1,0:T(8,128)(2,1)S(1)}, u32[]{:S(2)}, u32[]{:S(2)}) collective-permute-start(bf16[16,48,128]{2,1,0:T(8,128)(2,1)S(1)} %fusion.1), channel_id=1, source_target_pairs={{0,4},{1,5},{2,6},{3,7},{4,0},{5,1},{6,2},{7,3},{8,12},{9,13},{10,... | collective-permute-start | bytes 589832 | tf_op jit(solution)/shard_map/ppermute | solution.py:167
  60.0 11.9 %collective-permute-start.8 = (bf16[16,48,128]{2,1,0:T(8,128)(2,1)S(1)}, bf16[16,48,128]{2,1,0:T(8,128)(2,1)S(1)}, u32[]{:S(2)}, u32[]{:S(2)}) collective-permute-start(bf16[16,48,128]{2,1,0:T(8,128)(2,1)S(1)} %fusion.3), channel_id=1, source_target_pairs={{0,8},{1,9},{2,10},{3,11},{4,12},{5,13},{6,14},{7,15},{8,0},{9,1},... | collective-permute-start | bytes 589832 | tf_op jit(solution)/shard_map/ppermute | solution.py:167
  72.0 1.7 %collective-permute-start.9 = (bf16[16,48,128]{2,1,0:T(8,128)(2,1)S(1)}, bf16[16,48,128]{2,1,0:T(8,128)(2,1)S(1)}, u32[]{:S(2)}, u32[]{:S(2)}) collective-permute-start(bf16[16,48,128]{2,1,0:T(8,128)(2,1)S(1)} %get-tuple-element.10.coef_own), channel_id=1, source_target_pairs={{0,1},{1,0},{2,3},{3,2},{4,5},{5,4},{6,7},{7,6},{8,9},{9,8},{10,11... | collective-permute-start | bytes 589832 | tf_op jit(solution)/shard_map/ppermute | solution.py:167

commit v2 on v0

v2 whole, which is shorter than its diff:
```python
import functools

import jax
import jax.numpy as jnp
from jax import lax
from jax.experimental import pallas as pl
from jax.experimental.pallas import tpu as pltpu
from jax.sharding import PartitionSpec as P

F32 = jnp.float32
BF16 = jnp.bfloat16
NT = (((1,), (1,)), ((), ()))
NN = (((1,), (0,)), ((), ()))
PAIRS = 8
HEAD = 4
MIB = 2**20


def divide(x, by):
    if by & (by - 1) == 0:
        return lax.shift_right_logical(x, by.bit_length() - 1), x & (by - 1)
    return lax.div(x, by), lax.rem(x, by)


def place(axis):
    index = lax.axis_index(axis)
    return index & 1, lax.shift_right_logical(index, 1) & 1


def row_of(a, own, quarter, first, second):
    owner, rest = divide(a, own)
    return (
        (((owner & 1) ^ first) * 2 + ((lax.shift_right_logical(owner, 1) & 1) ^ second)) * quarter
        + lax.shift_right_logical(owner, 2) * own
        + rest
    )


def list_tails(live, slots, blocks, per_block):
    def block(b, total):
        pairs = lax.shift_right_logical(live[b] + 1, 1)

        def one(p, total):
            slots[total] = b * per_block + 2 * p
            return total + 1

        return lax.fori_loop(HEAD, pairs, one, total)

    total = lax.fori_loop(0, blocks, block, 0)
    for p in range(PAIRS):
        slots[total + p] = 0
    return total


def describe(slot, valid, live, screen, dead, own, quarter, bits):
    b, t = divide(slot, screen.shape[1])
    rows = []
    for k in (0, 1):
        row = row_of(screen[b, t + k], own, quarter, *bits)
        ok = t + k < live[b]
        rows.append(jnp.where(ok if valid is None else ok & valid, row, dead))
    return slot, b, rows


def chunks(live, screen, slots, total, dead, own, quarter, bits, ready_heads, ready_tails, work):
    blocks, per_block = screen.shape
    step = PAIRS // HEAD

    def head(c, _):
        ready_heads(c * step, step)
        entries = []
        for p in range(PAIRS):
            slot = (c * step + p // HEAD) * per_block + 2 * (p % HEAD)
            entries.append(describe(slot, None, live, screen, dead, own, quarter, bits))
        work(entries)
        return 0

    lax.fori_loop(0, blocks // step, head, 0)

    def tail(c, waited):
        last, _ = divide(slots[jnp.minimum(c * PAIRS + PAIRS - 1, total - 1)], per_block)
        waited = ready_tails(waited, last + 1)
        entries = []
        for p in range(PAIRS):
            i = c * PAIRS + p
            entries.append(describe(slots[i], i < total, live, screen, dead, own, quarter, bits))
        work(entries)
        return waited

    lax.fori_loop(0, lax.shift_right_logical(total + PAIRS - 1, PAIRS.bit_length() - 1), tail, 0)


def gamma_kernel(own, axis, live_h, screen_h, density_h, table_h, near, far, table, live, screen, slots, density, acc, small_sem, head_sem, tail_sem):
    blocks, per_block = screen.shape
    half, states, aux = near.shape
    bits = place(axis)
    small = [
        pltpu.make_async_copy(live_h, live, small_sem.at[0]),
        pltpu.make_async_copy(screen_h, screen, small_sem.at[1]),
        pltpu.make_async_copy(density_h, density, small_sem.at[2]),
    ]
    for copy in small:
        copy.start()

    def head_copy(b):
        part = pl.ds(pl.multiple_of(b * per_block * aux, 2 * aux), 2 * HEAD * aux)
        return pltpu.make_async_copy(table_h.at[part], table.at[part], head_sem.at[b])

    def tail_copy(b):
        rows = (lax.shift_right_logical(live[b] + 1, 1) - HEAD) * (2 * aux)
        part = pl.ds(pl.multiple_of(b * per_block * aux + 2 * HEAD * aux, 2 * aux), pl.multiple_of(rows, 2 * aux))
        return pltpu.make_async_copy(table_h.at[part], table.at[part], tail_sem.at[b])

    for b in range(blocks):
        head_copy(b).start()
    small[0].wait()
    for b in range(blocks):

        @pl.when(live[b] > 2 * HEAD)
        def _():
            tail_copy(b).start()

    acc[...] = jnp.zeros_like(acc)
    total = list_tails(live, slots, blocks, per_block)
    small[1].wait()
    small[2].wait()

    def ready_heads(b, count):
        for k in range(count):
            head_copy(b + k).wait()

    def ready_tails(begin, end):
        def one(b, _):
            @pl.when(live[b] > 2 * HEAD)
            def _():
                tail_copy(b).wait()

            return 0

        lax.fori_loop(begin, end, one, 0)
        return jnp.maximum(begin, end)

    def work(entries):
        products = []
        for slot, b, _ in entries:
            tile = table[pl.ds(pl.multiple_of(slot * aux, 2 * aux), 2 * aux), :]
            products.append(lax.dot_general(density[b], tile, NT, preferred_element_type=F32))
        for (_, _, rows), product in zip(entries, products):
            for k in (0, 1):
                acc[rows[k]] = acc[rows[k]] + product[:, k * aux : (k + 1) * aux]

    chunks(live, screen, slots, total, 2 * half, own, half // 2, bits, ready_heads, ready_tails, work)
    near[...] = acc[0:half]
    far[...] = acc[half : 2 * half]


def response_kernel(own, axis, live_h, screen_h, table, *refs):
    coefs, (sums, out, mine, live, screen, slots, coef, acc, small_sem) = refs[:4], refs[4:]
    blocks, per_block = screen.shape
    quarter, states, aux = coefs[0].shape
    bits = place(axis)
    small = [
        pltpu.make_async_copy(live_h, live, small_sem.at[0]),
        pltpu.make_async_copy(screen_h, screen, small_sem.at[1]),
    ]
    for copy in small:
        copy.start()
    acc[...] = jnp.zeros_like(acc)
    mine[...] = sums[pl.ds(lax.shift_right_logical(lax.axis_index(axis), 2) * own, own)]
    for k in range(4):
        coef[k * quarter : (k + 1) * quarter] = coefs[k][...]
    coef[4 * quarter] = jnp.zeros((states, aux), BF16)
    small[0].wait()
    total = list_tails(live, slots, blocks, per_block)
    small[1].wait()

    def work(entries):
        products = []
        for slot, b, rows in entries:
            tile = table[pl.ds(pl.multiple_of(slot * aux, 2 * aux), 2 * aux), :]
            picked = jnp.concatenate([coef[rows[0]], coef[rows[1]]], axis=1)
            products.append(lax.dot_general(picked, tile, NN, preferred_element_type=F32))
        for (_, b, _), product in zip(entries, products):
            acc[b] = acc[b] + product

    chunks(live, screen, slots, total, 4 * quarter, own, quarter, bits, lambda b, count: None, lambda begin, end: end, work)
    out[...] = acc[...].astype(out.dtype)


def metric_kernel(own, axis, *refs):
    gammas, (metric, near, far, high, low) = refs[:4], refs[4:]
    quarter, states, aux = gammas[0].shape
    rows = metric.shape[0]
    width = own * aux
    first, second = place(axis)

    def columns(h, k):
        owner = (h * 2 + ((k & 1) ^ second)) * 2 + ((k >> 1) ^ first)
        return pl.ds(pl.multiple_of(owner * width, width), width)

    fitted = jnp.zeros((states, rows), F32)
    for h in range(quarter // own):
        for k in range(4):
            part = columns(h, k)
            whole = metric[:, part]
            m_high = whole.astype(BF16)
            m_low = (whole - m_high.astype(F32)).astype(BF16)
            high[:, part] = m_high
            low[:, part] = m_low
            g = jnp.concatenate([gammas[k][h * own + j] for j in range(own)], axis=1)
            fitted += lax.dot_general(g, m_high, NT, preferred_element_type=F32)
            fitted += lax.dot_general(g, m_low, NT, preferred_element_type=F32)
    fitted_high = fitted.astype(BF16)
    fitted_low = (fitted - fitted_high.astype(F32)).astype(BF16)
    both = jnp.concatenate([fitted_high, fitted_low], axis=0)
    for h in range(quarter // own):
        for k in range(4):
            part = columns(h, k)
            c = lax.dot_general(both, high[:, part], NN, preferred_element_type=F32)
            c = c[:states] + c[states:] + lax.dot_general(fitted_high, low[:, part], NN, preferred_element_type=F32)
            out = near if k < 2 else far
            for j in range(own):
                out[(k & 1) * quarter + h * own + j] = c[:, j * aux : (j + 1) * aux]


def exchange(x, axis, devices, bit):
    return lax.ppermute(x, axis, [(j, j ^ bit) for j in range(devices)])


def summed(near, far, axis, devices):
    quarter = near.shape[0] // 2
    total = near + exchange(far, axis, devices, 1)
    total = total[:quarter] + exchange(total[quarter:].astype(BF16), axis, devices, 2).astype(F32)
    bit = 4
    while bit < devices:
        total = total + exchange(total.astype(BF16), axis, devices, bit).astype(F32)
        bit *= 2
    return total


def quarters(mine, axis, devices):
    other = exchange(mine, axis, devices, 2)
    return mine, other, exchange(mine, axis, devices, 1), exchange(other, axis, devices, 1)


def per_device(devices, density, three_index, live, screen, metric_inverse):
    axis = "pair"
    blocks, per_block = screen.shape
    states = density.shape[1]
    aux, pairs = three_index.shape[2:]
    own = metric_inverse.shape[0] // aux
    half = metric_inverse.shape[1] // aux // 2
    table = three_index.reshape(blocks * per_block * aux, pairs)
    anywhere = pl.BlockSpec(memory_space=pl.ANY)
    vmem = pl.BlockSpec(memory_space=pltpu.VMEM)
    lists = [
        pltpu.SMEM((blocks,), jnp.int32),
        pltpu.SMEM((blocks, per_block), jnp.int32),
        pltpu.SMEM((blocks * per_block // 2 + PAIRS,), jnp.int32),
    ]
    in_hbm = lambda x: pltpu.with_memory_space_constraint(x, pltpu.HBM)
    live, screen = in_hbm(live), in_hbm(screen)
    halves = [pltpu.VMEM((half, states, aux), F32)] * 2
    flops = 2 * blocks * per_block * aux * pairs * states

    near, far, table = pl.pallas_call(
        functools.partial(gamma_kernel, own, axis),
        out_shape=(*halves, pltpu.VMEM(table.shape, BF16)),
        in_specs=[anywhere] * 4,
        out_specs=(vmem, vmem, vmem),
        scratch_shapes=lists
        + [
            pltpu.VMEM(density.shape, BF16),
            pltpu.VMEM((2 * half + 1, states, aux), F32),
            pltpu.SemaphoreType.DMA((3,)),
            pltpu.SemaphoreType.DMA((blocks,)),
            pltpu.SemaphoreType.DMA((blocks,)),
        ],
        compiler_params=pltpu.CompilerParams(vmem_limit_bytes=16 * MIB),
        cost_estimate=pl.CostEstimate(flops=flops, bytes_accessed=table.size * 2, transcendentals=0),
        name="gamma",
    )(live, screen, in_hbm(density), in_hbm(table))
    gammas = quarters(summed(near, far, axis, devices).astype(BF16), axis, devices)

    near, far = pl.pallas_call(
        functools.partial(metric_kernel, own, axis),
        out_shape=tuple(halves),
        in_specs=[vmem] * 5,
        out_specs=(vmem, vmem),
        scratch_shapes=[pltpu.VMEM(metric_inverse.shape, BF16)] * 2,
        compiler_params=pltpu.CompilerParams(vmem_limit_bytes=24 * MIB),
        cost_estimate=pl.CostEstimate(flops=10 * metric_inverse.size * states, bytes_accessed=metric_inverse.size * 4, transcendentals=0),
        name="metric",
    )(*gammas, metric_inverse)
    total = summed(near, far, axis, devices)
    rounded = quarters(total.astype(BF16), axis, devices)

    return pl.pallas_call(
        functools.partial(response_kernel, own, axis),
        out_shape=(jax.ShapeDtypeStruct(density.shape, BF16), jax.ShapeDtypeStruct((own, states, aux), F32)),
        in_specs=[anywhere] * 2 + [vmem] * 6,
        out_specs=(vmem, vmem),
        scratch_shapes=lists
        + [
            pltpu.VMEM((2 * half + 1, states, aux), BF16),
            pltpu.VMEM(density.shape, F32),
            pltpu.SemaphoreType.DMA((2,)),
        ],
        compiler_params=pltpu.CompilerParams(vmem_limit_bytes=16 * MIB),
        cost_estimate=pl.CostEstimate(flops=flops, bytes_accessed=table.size * 2, transcendentals=0),
        name="response",
    )(live, screen, pltpu.with_memory_space_constraint(table, pltpu.VMEM), *rounded, total)


def solution(mesh):
    devices = mesh.shape["pair"]
    placed = (
        P(("groups", "pair"), None, None),
        P(("groups", "pair"), None, None, None),
        P(("groups", "pair")),
        P(("groups", "pair"), None),
        P("pair", None),
    )
    return jax.shard_map(
        functools.partial(per_device, devices),
        mesh=mesh,
        in_specs=placed,
        out_specs=(P(("groups", "pair"), None, None), P(("groups", "pair"), None, None)),
        check_vma=False,
    )
```

time: 238 us -> 65.3 us (0.27)
  waiting for transfers between devices: 145 us -> 33.6 us
  matrix products: 45.9 us -> 0 us
  blocking collectives: 20.5 us -> 0 us
  starting transfers between devices: 0.26 us -> 15.9 us
  Pallas kernels: 0 us -> 15.1 us
  between operations: 14.1 us -> 0.71 us
  local copies, waits for them, and re-layouts: 9.79 us -> 0.04 us
    psum x1 -> x0, waiting for transfers between devices: 89.8 us -> none  [per_device(): gamma_full = lax.psum(partial_gamma, 'pair')]
    reduce_scatter x1 -> x0, waiting for transfers between devices: 55.6 us -> none  [per_device(): lax.psum_scatter(jnp.einsum('xrqt,xsr->qst', metric, fitted, precision=la...]
    dot_general x5 -> x0, matrix products: 45.9 us -> none  [the longest x1 13.4 us: per_device(): jnp.einsum('bkrj,bsj->bksr', three_index, density, preferred_element_type...]
    ppermute x0 -> x14, waiting for transfers between devices: none -> 33.6 us  [exchange(): return lax.ppermute(x, axis, [(j, j ^ bit) for j in range(devices)])]
    all_gather x1 -> x0, blocking collectives: 20.5 us -> none  [per_device(): lax.all_gather(coefficients.astype(jnp.bfloat16), 'pair', axis=0, tiled=T...]
    ppermute x0 -> x14, starting transfers between devices: none -> 15.9 us  [exchange(): return lax.ppermute(x, axis, [(j, j ^ bit) for j in range(devices)])]
    pallas_call x0 -> x3, Pallas kernels: none -> 15.1 us  [the longest x1 6.99 us: per_device(): pl.pallas_call(functools.partial(gamma_kernel, own, axis), out_shape=(*ha...]
    unnamed x7 -> x2, local copies, waits for them, and re-layouts: 4.9 us -> 0.01 us
  transfers between devices with their start and end apart: 2 -> 14, of which waited for: 2 -> 12; matrix products, arithmetic and copies ran while one was open for 2% -> 0% of each run, Pallas kernels for 0% -> 0%
where the time goes in v2:
time: 65.3 us; the launch traced here: 65.7 us
  waiting for transfers between devices  33.6 us (51%)
  starting transfers between devices  15.9 us (24%)
  Pallas kernels  15.1 us (23%)
  between operations  0.71 us (1%)
    ppermute x14, waiting for transfers between devices, exchange(): return lax.ppermute(x, axis, [(j, j ^ bit) for j in range(devices)])  33.6 us
    ppermute x14, starting transfers between devices, exchange(): return lax.ppermute(x, axis, [(j, j ^ bit) for j in range(devices)])  15.9 us
    pallas_call x1, Pallas kernels, per_device(): pl.pallas_call(functools.partial(gamma_kernel, own, axis), out_shape=(*ha...  6.99 us
    pallas_call x1, Pallas kernels, per_device(): pl.pallas_call(functools.partial(response_kernel, own, axis), out_shape=(...  4.84 us
    pallas_call x1, Pallas kernels, per_device(): pl.pallas_call(functools.partial(metric_kernel, own, axis), out_shape=tup...  3.28 us
  transfers between devices with their start and end apart: 14, of which 12 were waited for; matrix products, arithmetic and copies ran while one was open for 0% of the time, Pallas kernels for 0%

profile of v2, /device:TPU:0, one launch (start us, length us, event | category | flops | bytes accessed | tf_op | source)
XLA Modules:
  0.0 65.7 jit_solution(11716987444643992291)
XLA Ops:
  0.6 0.0 copy-start
  0.6 7.0 %gamma.1 = (f32[16,48,128]{2,1,0:T(8,128)S(1)}, f32[16,48,128]{2,1,0:T(8,128)S(1)}, bf16[32768,256]{1,0:T(8,128)(2,1)S(1)}) custom-call(s32[8]{0:T(128)} %live_h.3, s32[8,32]{1,0:T(8,128)} %screen_h.3, bf16[8,48,256]{2,1,0:T(8,128)(2,1)} %density_h.1, bf16[32768,256]{1,0:T(8,128)(2,1)} %bitcast.1), custom_call_target="tpu_custom_call" | custom-call | flops 805306368 | bytes 16777216 | tf_op jit(solution)/shard_map/gamma/pallas_call | solution.py:266
  7.6 0.1 collective-permute-start
  7.7 1.7 %collective-permute-done = f32[16,48,128]{2,1,0:T(8,128)S(1)} collective-permute-done((f32[16,48,128]{2,1,0:T(8,128)S(1)}, f32[16,48,128]{2,1,0:T(8,128)S(1)}, u32[]{:S(2)}, u32[]{:S(2)}) %collective-permute-start) | collective-permute-done | bytes 393248 | tf_op jit(solution)/shard_map/ppermute | solution.py:227
  9.5 2.1 %collective-permute-start.1 = (bf16[8,48,128]{2,1,0:T(8,128)(2,1)S(1)}, bf16[8,48,128]{2,1,0:T(8,128)(2,1)S(1)}, u32[]{:S(2)}, u32[]{:S(2)}) collective-permute-start(bf16[8,48,128]{2,1,0:T(8,128)(2,1)S(1)} %slice.39), channel_id=1, source_target_pairs={{0,2},{1,3},{2,0},{3,1},{4,6},{5,7},{6,4},{7,5},{8,10},{9,11},{10,... | collective-permute-start | bytes 294920 | tf_op jit(solution)/shard_map/ppermute | solution.py:227
  11.6 3.3 %collective-permute-done.1 = bf16[8,48,128]{2,1,0:T(8,128)(2,1)S(1)} collective-permute-done((bf16[8,48,128]{2,1,0:T(8,128)(2,1)S(1)}, bf16[8,48,128]{2,1,0:T(8,128)(2,1)S(1)}, u32[]{:S(2)}, u32[]{:S(2)}) %collective-permute-start.1) | collective-permute-done | bytes 98336 | tf_op jit(solution)/shard_map/ppermute | solution.py:227
  14.9 1.4 %collective-permute-start.2 = (bf16[8,48,128]{2,1,0:T(8,128)(2,1)S(1)}, bf16[8,48,128]{2,1,0:T(8,128)(2,1)S(1)}, u32[]{:S(2)}, u32[]{:S(2)}) collective-permute-start(bf16[8,48,128]{2,1,0:T(8,128)(2,1)S(1)} %fusion.2), channel_id=1, source_target_pairs={{0,4},{1,5},{2,6},{3,7},{4,0},{5,1},{6,2},{7,3},{8,12},{9,13},{10,... | collective-permute-start | bytes 294920 | tf_op jit(solution)/shard_map/ppermute | solution.py:227
  16.3 3.3 %collective-permute-done.2 = bf16[8,48,128]{2,1,0:T(8,128)(2,1)S(1)} collective-permute-done((bf16[8,48,128]{2,1,0:T(8,128)(2,1)S(1)}, bf16[8,48,128]{2,1,0:T(8,128)(2,1)S(1)}, u32[]{:S(2)}, u32[]{:S(2)}) %collective-permute-start.2) | collective-permute-done | bytes 98336 | tf_op jit(solution)/shard_map/ppermute | solution.py:227
  19.6 4.0 %collective-permute-start.3 = (bf16[8,48,128]{2,1,0:T(8,128)(2,1)S(1)}, bf16[8,48,128]{2,1,0:T(8,128)(2,1)S(1)}, u32[]{:S(2)}, u32[]{:S(2)}) collective-permute-start(bf16[8,48,128]{2,1,0:T(8,128)(2,1)S(1)} %fusion), channel_id=1, source_target_pairs={{0,8},{1,9},{2,10},{3,11},{4,12},{5,13},{6,14},{7,15},{8,0},{9,1},... | collective-permute-start | bytes 294920 | tf_op jit(solution)/shard_map/ppermute | solution.py:227
  23.6 3.7 %collective-permute-done.3 = bf16[8,48,128]{2,1,0:T(8,128)(2,1)S(1)} collective-permute-done((bf16[8,48,128]{2,1,0:T(8,128)(2,1)S(1)}, bf16[8,48,128]{2,1,0:T(8,128)(2,1)S(1)}, u32[]{:S(2)}, u32[]{:S(2)}) %collective-permute-start.3) | collective-permute-done | bytes 98336 | tf_op jit(solution)/shard_map/ppermute | solution.py:227
  27.4 1.7 %collective-permute-start.4 = (bf16[8,48,128]{2,1,0:T(8,128)(2,1)S(1)}, bf16[8,48,128]{2,1,0:T(8,128)(2,1)S(1)}, u32[]{:S(2)}, u32[]{:S(2)}) collective-permute-start(bf16[8,48,128]{2,1,0:T(8,128)(2,1)S(1)} %add_convert_fusion.refs_0_), channel_id=1, source_target_pairs={{0,2},{1,3},{2,0},{3,1},{4,6},{5,7},{6,4},{7,5},{8,10},{9,11},{10,... | collective-permute-start | bytes 294920 | tf_op jit(solution)/shard_map/ppermute | solution.py:227
  29.1 0.0 collective-permute-start.5
  29.1 2.9 %collective-permute-done.4.refs_1_ = bf16[8,48,128]{2,1,0:T(8,128)(2,1)S(1)} collective-permute-done((bf16[8,48,128]{2,1,0:T(8,128)(2,1)S(1)}, bf16[8,48,128]{2,1,0:T(8,128)(2,1)S(1)}, u32[]{:S(2)}, u32[]{:S(2)}) %collective-permute-start.4) | collective-permute-done | bytes 98336 | tf_op jit(solution)/shard_map/ppermute | solution.py:227
  32.1 0.0 collective-permute-start.6
  32.1 0.0 collective-permute-done.5.refs_2_
  32.1 1.3 %collective-permute-done.6.refs_3_ = bf16[8,48,128]{2,1,0:T(8,128)(2,1)S(1)} collective-permute-done((bf16[8,48,128]{2,1,0:T(8,128)(2,1)S(1)}, bf16[8,48,128]{2,1,0:T(8,128)(2,1)S(1)}, u32[]{:S(2)}, u32[]{:S(2)}) %collective-permute-start.6) | collective-permute-done | bytes 98336 | tf_op jit(solution)/shard_map/ppermute | solution.py:227
  33.4 0.0 copy-done
  33.4 3.3 %metric.1 = (f32[16,48,128]{2,1,0:T(8,128)S(1)}, f32[16,48,128]{2,1,0:T(8,128)S(1)}) custom-call(bf16[8,48,128]{2,1,0:T(8,128)(2,1)S(1)} %add_convert_fusion.refs_0_, bf16[8,48,128]{2,1,0:T(8,128)(2,1)S(1)} %collective-permute-done.4.refs_1_, bf16[8,48,128]{2,1,0:T(8,128)(2,1)S(1)} %collective-permute-done.5.refs_2_, ...), custom_call_target="tpu_custom_call" | custom-call | flops 503316480 | bytes 4194304 | tf_op jit(solution)/shard_map/metric/pallas_call | solution.py:285
  36.7 0.2 collective-permute-start.7
  36.8 1.6 %collective-permute-done.7 = f32[16,48,128]{2,1,0:T(8,128)S(1)} collective-permute-done((f32[16,48,128]{2,1,0:T(8,128)S(1)}, f32[16,48,128]{2,1,0:T(8,128)S(1)}, u32[]{:S(2)}, u32[]{:S(2)}) %collective-permute-start.7) | collective-permute-done | bytes 393248 | tf_op jit(solution)/shard_map/ppermute | solution.py:227
  38.5 1.7 %collective-permute-start.8 = (bf16[8,48,128]{2,1,0:T(8,128)(2,1)S(1)}, bf16[8,48,128]{2,1,0:T(8,128)(2,1)S(1)}, u32[]{:S(2)}, u32[]{:S(2)}) collective-permute-start(bf16[8,48,128]{2,1,0:T(8,128)(2,1)S(1)} %slice.38), channel_id=1, source_target_pairs={{0,2},{1,3},{2,0},{3,1},{4,6},{5,7},{6,4},{7,5},{8,10},{9,11},{10,... | collective-permute-start | bytes 294920 | tf_op jit(solution)/shard_map/ppermute | solution.py:227
  40.2 3.2 %collective-permute-done.8 = bf16[8,48,128]{2,1,0:T(8,128)(2,1)S(1)} collective-permute-done((bf16[8,48,128]{2,1,0:T(8,128)(2,1)S(1)}, bf16[8,48,128]{2,1,0:T(8,128)(2,1)S(1)}, u32[]{:S(2)}, u32[]{:S(2)}) %collective-permute-start.8) | collective-permute-done | bytes 98336 | tf_op jit(solution)/shard_map/ppermute | solution.py:227
  43.4 0.8 %collective-permute-start.9 = (bf16[8,48,128]{2,1,0:T(8,128)(2,1)S(1)}, bf16[8,48,128]{2,1,0:T(8,128)(2,1)S(1)}, u32[]{:S(2)}, u32[]{:S(2)}) collective-permute-start(bf16[8,48,128]{2,1,0:T(8,128)(2,1)S(1)} %fusion.3), channel_id=1, source_target_pairs={{0,4},{1,5},{2,6},{3,7},{4,0},{5,1},{6,2},{7,3},{8,12},{9,13},{10,... | collective-permute-start | bytes 294920 | tf_op jit(solution)/shard_map/ppermute | solution.py:227
  44.2 3.9 %collective-permute-done.9 = bf16[8,48,128]{2,1,0:T(8,128)(2,1)S(1)} collective-permute-done((bf16[8,48,128]{2,1,0:T(8,128)(2,1)S(1)}, bf16[8,48,128]{2,1,0:T(8,128)(2,1)S(1)}, u32[]{:S(2)}, u32[]{:S(2)}) %collective-permute-start.9) | collective-permute-done | bytes 98336 | tf_op jit(solution)/shard_map/ppermute | solution.py:227
  48.1 2.1 %collective-permute-start.10 = (bf16[8,48,128]{2,1,0:T(8,128)(2,1)S(1)}, bf16[8,48,128]{2,1,0:T(8,128)(2,1)S(1)}, u32[]{:S(2)}, u32[]{:S(2)}) collective-permute-start(bf16[8,48,128]{2,1,0:T(8,128)(2,1)S(1)} %fusion.1), channel_id=1, source_target_pairs={{0,8},{1,9},{2,10},{3,11},{4,12},{5,13},{6,14},{7,15},{8,0},{9,1},... | collective-permute-start | bytes 294920 | tf_op jit(solution)/shard_map/ppermute | solution.py:227
  50.3 4.5 %collective-permute-done.10 = bf16[8,48,128]{2,1,0:T(8,128)(2,1)S(1)} collective-permute-done((bf16[8,48,128]{2,1,0:T(8,128)(2,1)S(1)}, bf16[8,48,128]{2,1,0:T(8,128)(2,1)S(1)}, u32[]{:S(2)}, u32[]{:S(2)}) %collective-permute-start.10) | collective-permute-done | bytes 98336 | tf_op jit(solution)/shard_map/ppermute | solution.py:227
  54.8 1.8 %collective-permute-start.11 = (bf16[8,48,128]{2,1,0:T(8,128)(2,1)S(1)}, bf16[8,48,128]{2,1,0:T(8,128)(2,1)S(1)}, u32[]{:S(2)}, u32[]{:S(2)}) collective-permute-start(bf16[8,48,128]{2,1,0:T(8,128)(2,1)S(1)} %get-tuple-element.12.refs_0_), channel_id=1, source_target_pairs={{0,2},{1,3},{2,0},{3,1},{4,6},{5,7},{6,4},{7,5},{8,10},{9,11},{10,... | collective-permute-start | bytes 294920 | tf_op jit(solution)/shard_map/ppermute | solution.py:227
  56.6 0.0 collective-permute-start.12
  56.6 2.9 %collective-permute-done.11.refs_1_ = bf16[8,48,128]{2,1,0:T(8,128)(2,1)S(1)} collective-permute-done((bf16[8,48,128]{2,1,0:T(8,128)(2,1)S(1)}, bf16[8,48,128]{2,1,0:T(8,128)(2,1)S(1)}, u32[]{:S(2)}, u32[]{:S(2)}) %collective-permute-start.11) | collective-permute-done | bytes 98336 | tf_op jit(solution)/shard_map/ppermute | solution.py:227
  59.5 0.0 collective-permute-start.13
  59.5 0.0 collective-permute-done.12.refs_2_
  59.5 1.3 %collective-permute-done.13.refs_3_ = bf16[8,48,128]{2,1,0:T(8,128)(2,1)S(1)} collective-permute-done((bf16[8,48,128]{2,1,0:T(8,128)(2,1)S(1)}, bf16[8,48,128]{2,1,0:T(8,128)(2,1)S(1)}, u32[]{:S(2)}, u32[]{:S(2)}) %collective-permute-start.13) | collective-permute-done | bytes 98336 | tf_op jit(solution)/shard_map/ppermute | solution.py:227
  60.8 4.8 %response.1 = (bf16[8,48,256]{2,1,0:T(8,128)(2,1)}, f32[2,48,128]{2,1,0:T(8,128)}) custom-call(s32[8]{0:T(128)} %live_h.3, s32[8,32]{1,0:T(8,128)} %screen_h.3, bf16[32768,256]{1,0:T(8,128)(2,1)S(1)} %get-tuple-element.7.table, bf16[8,48,128]{2,1,0:T(8,128)(2,1)S(1)} %get-tuple-element.12.refs_0_, bf16[8,48,128]{2,1,0:T(8,128)(2,1)S(1)} %collective-permute-done.11.refs_1_, ...), custom_call_target="tpu_custom_call" | custom-call | flops 805306368 | bytes 16777216 | tf_op jit(solution)/shard_map/response/pallas_call | solution.py:298
  (10 shorter events, 0.3 us)
Async XLA Ops:
  0.6 32.7 %copy-start = (f32[256,4096]{1,0:T(8,128)S(1)}, f32[256,4096]{1,0:T(8,128)}, u32[]{:S(2)}) copy-start(f32[256,4096]{1,0:T(8,128)} %refs_4_.1) | copy-start | bytes 12582916
  7.6 1.8 %collective-permute-start = (f32[16,48,128]{2,1,0:T(8,128)S(1)}, f32[16,48,128]{2,1,0:T(8,128)S(1)}, u32[]{:S(2)}, u32[]{:S(2)}) collective-permute-start(f32[16,48,128]{2,1,0:T(8,128)S(1)} %get-tuple-element.9), channel_id=1, source_target_pairs={{0,1},{1,0},{2,3},{3,2},{4,5},{5,4},{6,7},{7,6},{8,9},{9,8},{10,11... | collective-permute-start | bytes 1179656 | tf_op jit(solution)/shard_map/ppermute | solution.py:227
  9.5 5.4 %collective-permute-start.1 = (bf16[8,48,128]{2,1,0:T(8,128)(2,1)S(1)}, bf16[8,48,128]{2,1,0:T(8,128)(2,1)S(1)}, u32[]{:S(2)}, u32[]{:S(2)}) collective-permute-start(bf16[8,48,128]{2,1,0:T(8,128)(2,1)S(1)} %slice.39), channel_id=1, source_target_pairs={{0,2},{1,3},{2,0},{3,1},{4,6},{5,7},{6,4},{7,5},{8,10},{9,11},{10,... | collective-permute-start | bytes 294920 | tf_op jit(solution)/shard_map/ppermute | solution.py:227
  14.9 4.7 %collective-permute-start.2 = (bf16[8,48,128]{2,1,0:T(8,128)(2,1)S(1)}, bf16[8,48,128]{2,1,0:T(8,128)(2,1)S(1)}, u32[]{:S(2)}, u32[]{:S(2)}) collective-permute-start(bf16[8,48,128]{2,1,0:T(8,128)(2,1)S(1)} %fusion.2), channel_id=1, source_target_pairs={{0,4},{1,5},{2,6},{3,7},{4,0},{5,1},{6,2},{7,3},{8,12},{9,13},{10,... | collective-permute-start | bytes 294920 | tf_op jit(solution)/shard_map/ppermute | solution.py:227
  19.6 7.7 %collective-permute-start.3 = (bf16[8,48,128]{2,1,0:T(8,128)(2,1)S(1)}, bf16[8,48,128]{2,1,0:T(8,128)(2,1)S(1)}, u32[]{:S(2)}, u32[]{:S(2)}) collective-permute-start(bf16[8,48,128]{2,1,0:T(8,128)(2,1)S(1)} %fusion), channel_id=1, source_target_pairs={{0,8},{1,9},{2,10},{3,11},{4,12},{5,13},{6,14},{7,15},{8,0},{9,1},... | collective-permute-start | bytes 294920 | tf_op jit(solution)/shard_map/ppermute | solution.py:227
  27.4 4.7 %collective-permute-start.4 = (bf16[8,48,128]{2,1,0:T(8,128)(2,1)S(1)}, bf16[8,48,128]{2,1,0:T(8,128)(2,1)S(1)}, u32[]{:S(2)}, u32[]{:S(2)}) collective-permute-start(bf16[8,48,128]{2,1,0:T(8,128)(2,1)S(1)} %add_convert_fusion.refs_0_), channel_id=1, source_target_pairs={{0,2},{1,3},{2,0},{3,1},{4,6},{5,7},{6,4},{7,5},{8,10},{9,11},{10,... | collective-permute-start | bytes 294920 | tf_op jit(solution)/shard_map/ppermute | solution.py:227
  29.1 2.9 %collective-permute-start.5 = (bf16[8,48,128]{2,1,0:T(8,128)(2,1)S(1)}, bf16[8,48,128]{2,1,0:T(8,128)(2,1)S(1)}, u32[]{:S(2)}, u32[]{:S(2)}) collective-permute-start(bf16[8,48,128]{2,1,0:T(8,128)(2,1)S(1)} %add_convert_fusion.refs_0_), channel_id=1, source_target_pairs={{0,1},{1,0},{2,3},{3,2},{4,5},{5,4},{6,7},{7,6},{8,9},{9,8},{10,11... | collective-permute-start | bytes 294920 | tf_op jit(solution)/shard_map/ppermute | solution.py:227
  32.1 1.3 %collective-permute-start.6 = (bf16[8,48,128]{2,1,0:T(8,128)(2,1)S(1)}, bf16[8,48,128]{2,1,0:T(8,128)(2,1)S(1)}, u32[]{:S(2)}, u32[]{:S(2)}) collective-permute-start(bf16[8,48,128]{2,1,0:T(8,128)(2,1)S(1)} %collective-permute-done.4.refs_1_), channel_id=1, source_target_pairs={{0,1},{1,0},{2,3},{3,2},{4,5},{5,4},{6,7},{7,6},{8,9},{9,8},{10,11... | collective-permute-start | bytes 294920 | tf_op jit(solution)/shard_map/ppermute | solution.py:227
  36.7 1.8 %collective-permute-start.7 = (f32[16,48,128]{2,1,0:T(8,128)S(1)}, f32[16,48,128]{2,1,0:T(8,128)S(1)}, u32[]{:S(2)}, u32[]{:S(2)}) collective-permute-start(f32[16,48,128]{2,1,0:T(8,128)S(1)} %get-tuple-element.11), channel_id=1, source_target_pairs={{0,1},{1,0},{2,3},{3,2},{4,5},{5,4},{6,7},{7,6},{8,9},{9,8},{10,11... | collective-permute-start | bytes 1179656 | tf_op jit(solution)/shard_map/ppermute | solution.py:227
  38.5 4.9 %collective-permute-start.8 = (bf16[8,48,128]{2,1,0:T(8,128)(2,1)S(1)}, bf16[8,48,128]{2,1,0:T(8,128)(2,1)S(1)}, u32[]{:S(2)}, u32[]{:S(2)}) collective-permute-start(bf16[8,48,128]{2,1,0:T(8,128)(2,1)S(1)} %slice.38), channel_id=1, source_target_pairs={{0,2},{1,3},{2,0},{3,1},{4,6},{5,7},{6,4},{7,5},{8,10},{9,11},{10,... | collective-permute-start | bytes 294920 | tf_op jit(solution)/shard_map/ppermute | solution.py:227
  43.4 4.7 %collective-permute-start.9 = (bf16[8,48,128]{2,1,0:T(8,128)(2,1)S(1)}, bf16[8,48,128]{2,1,0:T(8,128)(2,1)S(1)}, u32[]{:S(2)}, u32[]{:S(2)}) collective-permute-start(bf16[8,48,128]{2,1,0:T(8,128)(2,1)S(1)} %fusion.3), channel_id=1, source_target_pairs={{0,4},{1,5},{2,6},{3,7},{4,0},{5,1},{6,2},{7,3},{8,12},{9,13},{10,... | collective-permute-start | bytes 294920 | tf_op jit(solution)/shard_map/ppermute | solution.py:227
  48.1 6.6 %collective-permute-start.10 = (bf16[8,48,128]{2,1,0:T(8,128)(2,1)S(1)}, bf16[8,48,128]{2,1,0:T(8,128)(2,1)S(1)}, u32[]{:S(2)}, u32[]{:S(2)}) collective-permute-start(bf16[8,48,128]{2,1,0:T(8,128)(2,1)S(1)} %fusion.1), channel_id=1, source_target_pairs={{0,8},{1,9},{2,10},{3,11},{4,12},{5,13},{6,14},{7,15},{8,0},{9,1},... | collective-permute-start | bytes 294920 | tf_op jit(solution)/shard_map/ppermute | solution.py:227
  54.8 4.7 %collective-permute-start.11 = (bf16[8,48,128]{2,1,0:T(8,128)(2,1)S(1)}, bf16[8,48,128]{2,1,0:T(8,128)(2,1)S(1)}, u32[]{:S(2)}, u32[]{:S(2)}) collective-permute-start(bf16[8,48,128]{2,1,0:T(8,128)(2,1)S(1)} %get-tuple-element.12.refs_0_), channel_id=1, source_target_pairs={{0,2},{1,3},{2,0},{3,1},{4,6},{5,7},{6,4},{7,5},{8,10},{9,11},{10,... | collective-permute-start | bytes 294920 | tf_op jit(solution)/shard_map/ppermute | solution.py:227
  56.6 2.9 %collective-permute-start.12 = (bf16[8,48,128]{2,1,0:T(8,128)(2,1)S(1)}, bf16[8,48,128]{2,1,0:T(8,128)(2,1)S(1)}, u32[]{:S(2)}, u32[]{:S(2)}) collective-permute-start(bf16[8,48,128]{2,1,0:T(8,128)(2,1)S(1)} %get-tuple-element.12.refs_0_), channel_id=1, source_target_pairs={{0,1},{1,0},{2,3},{3,2},{4,5},{5,4},{6,7},{7,6},{8,9},{9,8},{10,11... | collective-permute-start | bytes 294920 | tf_op jit(solution)/shard_map/ppermute | solution.py:227
  59.5 1.3 %collective-permute-start.13 = (bf16[8,48,128]{2,1,0:T(8,128)(2,1)S(1)}, bf16[8,48,128]{2,1,0:T(8,128)(2,1)S(1)}, u32[]{:S(2)}, u32[]{:S(2)}) collective-permute-start(bf16[8,48,128]{2,1,0:T(8,128)(2,1)S(1)} %collective-permute-done.11.refs_1_), channel_id=1, source_target_pairs={{0,1},{1,0},{2,3},{3,2},{4,5},{5,4},{6,7},{7,6},{8,9},{9,8},{10,11... | collective-permute-start | bytes 294920 | tf_op jit(solution)/shard_map/ppermute | solution.py:227

commit v3 on v2

--- a/solution.py
+++ b/solution.py
@@ -11,7 +11,8 @@
 BF16 = jnp.bfloat16
 NT = (((1,), (1,)), ((), ()))
 NN = (((1,), (0,)), ((), ()))
-PAIRS = 8
+PAIRS = 32
+LEAST = 8
 HEAD = 4
 MIB = 2**20
 
@@ -64,12 +65,12 @@
 
 def chunks(live, screen, slots, total, dead, own, quarter, bits, ready_heads, ready_tails, work):
     blocks, per_block = screen.shape
-    step = PAIRS // HEAD
+    step = max(1, min(blocks, PAIRS // HEAD))
 
     def head(c, _):
         ready_heads(c * step, step)
         entries = []
-        for p in range(PAIRS):
+        for p in range(step * HEAD):
             slot = (c * step + p // HEAD) * per_block + 2 * (p % HEAD)
             entries.append(describe(slot, None, live, screen, dead, own, quarter, bits))
         work(entries)
@@ -77,18 +78,28 @@
 
     lax.fori_loop(0, blocks // step, head, 0)
 
-    def tail(c, waited):
-        last, _ = divide(slots[jnp.minimum(c * PAIRS + PAIRS - 1, total - 1)], per_block)
+    def tail(size, begin, waited):
+        last, _ = divide(slots[jnp.minimum(begin + size - 1, total - 1)], per_block)
         waited = ready_tails(waited, last + 1)
         entries = []
-        for p in range(PAIRS):
-            i = c * PAIRS + p
+        for p in range(size):
+            i = begin + p
             entries.append(describe(slots[i], i < total, live, screen, dead, own, quarter, bits))
         work(entries)
         return waited
 
-    lax.fori_loop(0, lax.shift_right_logical(total + PAIRS - 1, PAIRS.bit_length() - 1), tail, 0)
-
+    whole = lax.shift_right_logical(total, PAIRS.bit_length() - 1)
+    waited = lax.fori_loop(0, whole, lambda c, waited: tail(PAIRS, c * PAIRS, waited), 0)
+    begin, size = whole * PAIRS, PAIRS // 2
+    while size >= LEAST:
+        left = total - begin
+        if size > LEAST:
+            more = (left >= size).astype(jnp.int32)
+        else:
+            more = lax.div(left + size - 1, size)
+        waited = lax.fori_loop(0, more, lambda c, waited, begin=begin, size=size: tail(size, begin + c * size, waited), waited)
+        begin = begin + more * size
+        size //= 2
 
 def gamma_kernel(own, axis, live_h, screen_h, density_h, table_h, near, far, table, live, screen, slots, density, acc, small_sem, head_sem, tail_sem):
     blocks, per_block = screen.shape
@@ -259,7 +270,6 @@
         pltpu.SMEM((blocks * per_block // 2 + PAIRS,), jnp.int32),
     ]
     in_hbm = lambda x: pltpu.with_memory_space_constraint(x, pltpu.HBM)
-    live, screen = in_hbm(live), in_hbm(screen)
     halves = [pltpu.VMEM((half, states, aux), F32)] * 2
     flops = 2 * blocks * per_block * aux * pairs * states
 
@@ -279,7 +289,7 @@
         compiler_params=pltpu.CompilerParams(vmem_limit_bytes=16 * MIB),
         cost_estimate=pl.CostEstimate(flops=flops, bytes_accessed=table.size * 2, transcendentals=0),
         name="gamma",
-    )(live, screen, in_hbm(density), in_hbm(table))
+    )(in_hbm(live), in_hbm(screen), in_hbm(density), in_hbm(table))
     gammas = quarters(summed(near, far, axis, devices).astype(BF16), axis, devices)
 
     near, far = pl.pallas_call(

time: 65.3 us -> 63.3 us (0.969)
  Pallas kernels: 15.1 us -> 11.8 us
  starting transfers between devices: 15.9 us -> 18 us
  waiting for transfers between devices: 33.6 us -> 32.3 us
    ppermute x14, starting transfers between devices: 15.9 us -> 18 us  [exchange(): return lax.ppermute(x, axis, [(j, j ^ bit) for j in range(devices)])]
    pallas_call x1, Pallas kernels: 4.84 us -> 3.19 us  [per_device(): pl.pallas_call(functools.partial(response_kernel, own, axis), out_shape=(...]
    pallas_call x1, Pallas kernels: 6.99 us -> 5.34 us  [per_device(): pl.pallas_call(functools.partial(gamma_kernel, own, axis), out_shape=(*ha...]
    ppermute x14, waiting for transfers between devices: 33.6 us -> 32.3 us  [exchange(): return lax.ppermute(x, axis, [(j, j ^ bit) for j in range(devices)])]
where the time goes in v3:
time: 63.3 us; the launch traced here: 63.2 us
  waiting for transfers between devices  32.3 us (51%)
  starting transfers between devices  18 us (28%)
  Pallas kernels  11.8 us (19%)
  between operations  0.72 us (1%)
    ppermute x14, waiting for transfers between devices, exchange(): return lax.ppermute(x, axis, [(j, j ^ bit) for j in range(devices)])  32.3 us
    ppermute x14, starting transfers between devices, exchange(): return lax.ppermute(x, axis, [(j, j ^ bit) for j in range(devices)])  18 us
    pallas_call x1, Pallas kernels, per_device(): pl.pallas_call(functools.partial(gamma_kernel, own, axis), out_shape=(*ha...  5.34 us
    pallas_call x1, Pallas kernels, per_device(): pl.pallas_call(functools.partial(metric_kernel, own, axis), out_shape=tup...  3.28 us
    pallas_call x1, Pallas kernels, per_device(): pl.pallas_call(functools.partial(response_kernel, own, axis), out_shape=(...  3.19 us
  transfers between devices with their start and end apart: 14, of which 12 were waited for; matrix products, arithmetic and copies ran while one was open for 0% of the time, Pallas kernels for 0%

profile of v3, /device:TPU:0, one launch (start us, length us, event | category | flops | bytes accessed | tf_op | source)
XLA Modules:
  0.0 63.2 jit_solution(2976981194814520478)
XLA Ops:
  0.6 0.0 copy-start.1
  0.6 0.0 copy-start.2
  0.7 0.0 copy-start
  0.7 5.3 %gamma.1 = (f32[16,48,128]{2,1,0:T(8,128)S(1)}, f32[16,48,128]{2,1,0:T(8,128)S(1)}, bf16[32768,256]{1,0:T(8,128)(2,1)S(1)}) custom-call(s32[8]{0:T(128)} %live_h.3, s32[8,32]{1,0:T(8,128)} %screen_h.3, bf16[8,48,256]{2,1,0:T(8,128)(2,1)} %density_h.1, bf16[32768,256]{1,0:T(8,128)(2,1)} %bitcast.1), custom_call_target="tpu_custom_call" | custom-call | flops 805306368 | bytes 16777216 | tf_op jit(solution)/shard_map/gamma/pallas_call | solution.py:276
  6.0 0.2 collective-permute-start
  6.2 1.6 %collective-permute-done = f32[16,48,128]{2,1,0:T(8,128)S(1)} collective-permute-done((f32[16,48,128]{2,1,0:T(8,128)S(1)}, f32[16,48,128]{2,1,0:T(8,128)S(1)}, u32[]{:S(2)}, u32[]{:S(2)}) %collective-permute-start) | collective-permute-done | bytes 393248 | tf_op jit(solution)/shard_map/ppermute | solution.py:238
  7.9 4.2 %collective-permute-start.1 = (bf16[8,48,128]{2,1,0:T(8,128)(2,1)S(1)}, bf16[8,48,128]{2,1,0:T(8,128)(2,1)S(1)}, u32[]{:S(2)}, u32[]{:S(2)}) collective-permute-start(bf16[8,48,128]{2,1,0:T(8,128)(2,1)S(1)} %slice.39), channel_id=1, source_target_pairs={{0,2},{1,3},{2,0},{3,1},{4,6},{5,7},{6,4},{7,5},{8,10},{9,11},{10,... | collective-permute-start | bytes 294920 | tf_op jit(solution)/shard_map/ppermute | solution.py:238
  12.0 3.1 %collective-permute-done.1 = bf16[8,48,128]{2,1,0:T(8,128)(2,1)S(1)} collective-permute-done((bf16[8,48,128]{2,1,0:T(8,128)(2,1)S(1)}, bf16[8,48,128]{2,1,0:T(8,128)(2,1)S(1)}, u32[]{:S(2)}, u32[]{:S(2)}) %collective-permute-start.1) | collective-permute-done | bytes 98336 | tf_op jit(solution)/shard_map/ppermute | solution.py:238
  15.2 2.1 %collective-permute-start.2 = (bf16[8,48,128]{2,1,0:T(8,128)(2,1)S(1)}, bf16[8,48,128]{2,1,0:T(8,128)(2,1)S(1)}, u32[]{:S(2)}, u32[]{:S(2)}) collective-permute-start(bf16[8,48,128]{2,1,0:T(8,128)(2,1)S(1)} %fusion.2), channel_id=1, source_target_pairs={{0,4},{1,5},{2,6},{3,7},{4,0},{5,1},{6,2},{7,3},{8,12},{9,13},{10,... | collective-permute-start | bytes 294920 | tf_op jit(solution)/shard_map/ppermute | solution.py:238
  17.3 2.6 %collective-permute-done.2 = bf16[8,48,128]{2,1,0:T(8,128)(2,1)S(1)} collective-permute-done((bf16[8,48,128]{2,1,0:T(8,128)(2,1)S(1)}, bf16[8,48,128]{2,1,0:T(8,128)(2,1)S(1)}, u32[]{:S(2)}, u32[]{:S(2)}) %collective-permute-start.2) | collective-permute-done | bytes 98336 | tf_op jit(solution)/shard_map/ppermute | solution.py:238
  19.9 2.6 %collective-permute-start.3 = (bf16[8,48,128]{2,1,0:T(8,128)(2,1)S(1)}, bf16[8,48,128]{2,1,0:T(8,128)(2,1)S(1)}, u32[]{:S(2)}, u32[]{:S(2)}) collective-permute-start(bf16[8,48,128]{2,1,0:T(8,128)(2,1)S(1)} %fusion), channel_id=1, source_target_pairs={{0,8},{1,9},{2,10},{3,11},{4,12},{5,13},{6,14},{7,15},{8,0},{9,1},... | collective-permute-start | bytes 294920 | tf_op jit(solution)/shard_map/ppermute | solution.py:238
  22.5 3.0 %collective-permute-done.3 = bf16[8,48,128]{2,1,0:T(8,128)(2,1)S(1)} collective-permute-done((bf16[8,48,128]{2,1,0:T(8,128)(2,1)S(1)}, bf16[8,48,128]{2,1,0:T(8,128)(2,1)S(1)}, u32[]{:S(2)}, u32[]{:S(2)}) %collective-permute-start.3) | collective-permute-done | bytes 98336 | tf_op jit(solution)/shard_map/ppermute | solution.py:238
  25.5 2.8 %collective-permute-start.4 = (bf16[8,48,128]{2,1,0:T(8,128)(2,1)S(1)}, bf16[8,48,128]{2,1,0:T(8,128)(2,1)S(1)}, u32[]{:S(2)}, u32[]{:S(2)}) collective-permute-start(bf16[8,48,128]{2,1,0:T(8,128)(2,1)S(1)} %add_convert_fusion.refs_0_), channel_id=1, source_target_pairs={{0,2},{1,3},{2,0},{3,1},{4,6},{5,7},{6,4},{7,5},{8,10},{9,11},{10,... | collective-permute-start | bytes 294920 | tf_op jit(solution)/shard_map/ppermute | solution.py:238
  28.4 0.0 collective-permute-start.5
  28.4 2.6 %collective-permute-done.4.refs_1_ = bf16[8,48,128]{2,1,0:T(8,128)(2,1)S(1)} collective-permute-done((bf16[8,48,128]{2,1,0:T(8,128)(2,1)S(1)}, bf16[8,48,128]{2,1,0:T(8,128)(2,1)S(1)}, u32[]{:S(2)}, u32[]{:S(2)}) %collective-permute-start.4) | collective-permute-done | bytes 98336 | tf_op jit(solution)/shard_map/ppermute | solution.py:238
  31.0 0.0 collective-permute-start.6
  31.0 0.0 collective-permute-done.5.refs_2_
  31.0 1.3 %collective-permute-done.6.refs_3_ = bf16[8,48,128]{2,1,0:T(8,128)(2,1)S(1)} collective-permute-done((bf16[8,48,128]{2,1,0:T(8,128)(2,1)S(1)}, bf16[8,48,128]{2,1,0:T(8,128)(2,1)S(1)}, u32[]{:S(2)}, u32[]{:S(2)}) %collective-permute-start.6) | collective-permute-done | bytes 98336 | tf_op jit(solution)/shard_map/ppermute | solution.py:238
  32.3 0.0 copy-done
  32.3 3.3 %metric.1 = (f32[16,48,128]{2,1,0:T(8,128)S(1)}, f32[16,48,128]{2,1,0:T(8,128)S(1)}) custom-call(bf16[8,48,128]{2,1,0:T(8,128)(2,1)S(1)} %add_convert_fusion.refs_0_, bf16[8,48,128]{2,1,0:T(8,128)(2,1)S(1)} %collective-permute-done.4.refs_1_, bf16[8,48,128]{2,1,0:T(8,128)(2,1)S(1)} %collective-permute-done.5.refs_2_, ...), custom_call_target="tpu_custom_call" | custom-call | flops 503316480 | bytes 4194304 | tf_op jit(solution)/shard_map/metric/pallas_call | solution.py:295
  35.6 0.2 collective-permute-start.7
  35.7 1.6 %collective-permute-done.7 = f32[16,48,128]{2,1,0:T(8,128)S(1)} collective-permute-done((f32[16,48,128]{2,1,0:T(8,128)S(1)}, f32[16,48,128]{2,1,0:T(8,128)S(1)}, u32[]{:S(2)}, u32[]{:S(2)}) %collective-permute-start.7) | collective-permute-done | bytes 393248 | tf_op jit(solution)/shard_map/ppermute | solution.py:238
  37.4 2.1 %collective-permute-start.8 = (bf16[8,48,128]{2,1,0:T(8,128)(2,1)S(1)}, bf16[8,48,128]{2,1,0:T(8,128)(2,1)S(1)}, u32[]{:S(2)}, u32[]{:S(2)}) collective-permute-start(bf16[8,48,128]{2,1,0:T(8,128)(2,1)S(1)} %slice.38), channel_id=1, source_target_pairs={{0,2},{1,3},{2,0},{3,1},{4,6},{5,7},{6,4},{7,5},{8,10},{9,11},{10,... | collective-permute-start | bytes 294920 | tf_op jit(solution)/shard_map/ppermute | solution.py:238
  39.5 3.1 %collective-permute-done.8 = bf16[8,48,128]{2,1,0:T(8,128)(2,1)S(1)} collective-permute-done((bf16[8,48,128]{2,1,0:T(8,128)(2,1)S(1)}, bf16[8,48,128]{2,1,0:T(8,128)(2,1)S(1)}, u32[]{:S(2)}, u32[]{:S(2)}) %collective-permute-start.8) | collective-permute-done | bytes 98336 | tf_op jit(solution)/shard_map/ppermute | solution.py:238
  42.6 1.0 %collective-permute-start.9 = (bf16[8,48,128]{2,1,0:T(8,128)(2,1)S(1)}, bf16[8,48,128]{2,1,0:T(8,128)(2,1)S(1)}, u32[]{:S(2)}, u32[]{:S(2)}) collective-permute-start(bf16[8,48,128]{2,1,0:T(8,128)(2,1)S(1)} %fusion.3), channel_id=1, source_target_pairs={{0,4},{1,5},{2,6},{3,7},{4,0},{5,1},{6,2},{7,3},{8,12},{9,13},{10,... | collective-permute-start | bytes 294920 | tf_op jit(solution)/shard_map/ppermute | solution.py:238
  43.7 3.6 %collective-permute-done.9 = bf16[8,48,128]{2,1,0:T(8,128)(2,1)S(1)} collective-permute-done((bf16[8,48,128]{2,1,0:T(8,128)(2,1)S(1)}, bf16[8,48,128]{2,1,0:T(8,128)(2,1)S(1)}, u32[]{:S(2)}, u32[]{:S(2)}) %collective-permute-start.9) | collective-permute-done | bytes 98336 | tf_op jit(solution)/shard_map/ppermute | solution.py:238
  47.3 1.6 %collective-permute-start.10 = (bf16[8,48,128]{2,1,0:T(8,128)(2,1)S(1)}, bf16[8,48,128]{2,1,0:T(8,128)(2,1)S(1)}, u32[]{:S(2)}, u32[]{:S(2)}) collective-permute-start(bf16[8,48,128]{2,1,0:T(8,128)(2,1)S(1)} %fusion.1), channel_id=1, source_target_pairs={{0,8},{1,9},{2,10},{3,11},{4,12},{5,13},{6,14},{7,15},{8,0},{9,1},... | collective-permute-start | bytes 294920 | tf_op jit(solution)/shard_map/ppermute | solution.py:238
  49.0 5.0 %collective-permute-done.10 = bf16[8,48,128]{2,1,0:T(8,128)(2,1)S(1)} collective-permute-done((bf16[8,48,128]{2,1,0:T(8,128)(2,1)S(1)}, bf16[8,48,128]{2,1,0:T(8,128)(2,1)S(1)}, u32[]{:S(2)}, u32[]{:S(2)}) %collective-permute-start.10) | collective-permute-done | bytes 98336 | tf_op jit(solution)/shard_map/ppermute | solution.py:238
  54.0 1.2 %collective-permute-start.11 = (bf16[8,48,128]{2,1,0:T(8,128)(2,1)S(1)}, bf16[8,48,128]{2,1,0:T(8,128)(2,1)S(1)}, u32[]{:S(2)}, u32[]{:S(2)}) collective-permute-start(bf16[8,48,128]{2,1,0:T(8,128)(2,1)S(1)} %get-tuple-element.12.refs_0_), channel_id=1, source_target_pairs={{0,2},{1,3},{2,0},{3,1},{4,6},{5,7},{6,4},{7,5},{8,10},{9,11},{10,... | collective-permute-start | bytes 294920 | tf_op jit(solution)/shard_map/ppermute | solution.py:238
  55.3 0.0 collective-permute-start.12
  55.3 3.4 %collective-permute-done.11.refs_1_ = bf16[8,48,128]{2,1,0:T(8,128)(2,1)S(1)} collective-permute-done((bf16[8,48,128]{2,1,0:T(8,128)(2,1)S(1)}, bf16[8,48,128]{2,1,0:T(8,128)(2,1)S(1)}, u32[]{:S(2)}, u32[]{:S(2)}) %collective-permute-start.11) | collective-permute-done | bytes 98336 | tf_op jit(solution)/shard_map/ppermute | solution.py:238
  58.7 0.0 collective-permute-start.13
  58.7 0.0 collective-permute-done.12.refs_2_
  58.7 1.3 %collective-permute-done.13.refs_3_ = bf16[8,48,128]{2,1,0:T(8,128)(2,1)S(1)} collective-permute-done((bf16[8,48,128]{2,1,0:T(8,128)(2,1)S(1)}, bf16[8,48,128]{2,1,0:T(8,128)(2,1)S(1)}, u32[]{:S(2)}, u32[]{:S(2)}) %collective-permute-start.13) | collective-permute-done | bytes 98336 | tf_op jit(solution)/shard_map/ppermute | solution.py:238
  60.0 0.0 copy-done.1
  60.0 0.0 copy-done.2
  60.0 3.2 %response.1 = (bf16[8,48,256]{2,1,0:T(8,128)(2,1)}, f32[2,48,128]{2,1,0:T(8,128)}) custom-call(s32[8]{0:T(128)S(1)} %copy-done.2, s32[8,32]{1,0:T(8,128)S(1)} %copy-done.1, bf16[32768,256]{1,0:T(8,128)(2,1)S(1)} %get-tuple-element.7.table, bf16[8,48,128]{2,1,0:T(8,128)(2,1)S(1)} %get-tuple-element.12.refs_0_, ...), custom_call_target="tpu_custom_call" | custom-call | flops 805306368 | bytes 16777216 | tf_op jit(solution)/shard_map/response/pallas_call | solution.py:308
  (10 shorter events, 0.3 us)
Async XLA Ops:
  0.6 59.4 %copy-start.1 = (s32[8,32]{1,0:T(8,128)S(1)}, s32[8,32]{1,0:T(8,128)}, u32[]{:S(2)}) copy-start(s32[8,32]{1,0:T(8,128)} %screen_h.3) | copy-start | bytes 3076
  0.6 59.4 %copy-start.2 = (s32[8]{0:T(128)S(1)}, s32[8]{0:T(128)}, u32[]{:S(2)}) copy-start(s32[8]{0:T(128)} %live_h.3) | copy-start | bytes 100
  0.7 31.6 %copy-start = (f32[256,4096]{1,0:T(8,128)S(1)}, f32[256,4096]{1,0:T(8,128)}, u32[]{:S(2)}) copy-start(f32[256,4096]{1,0:T(8,128)} %refs_4_.1) | copy-start | bytes 12582916
  6.0 1.8 %collective-permute-start = (f32[16,48,128]{2,1,0:T(8,128)S(1)}, f32[16,48,128]{2,1,0:T(8,128)S(1)}, u32[]{:S(2)}, u32[]{:S(2)}) collective-permute-start(f32[16,48,128]{2,1,0:T(8,128)S(1)} %get-tuple-element.9), channel_id=1, source_target_pairs={{0,1},{1,0},{2,3},{3,2},{4,5},{5,4},{6,7},{7,6},{8,9},{9,8},{10,11... | collective-permute-start | bytes 1179656 | tf_op jit(solution)/shard_map/ppermute | solution.py:238
  7.9 7.3 %collective-permute-start.1 = (bf16[8,48,128]{2,1,0:T(8,128)(2,1)S(1)}, bf16[8,48,128]{2,1,0:T(8,128)(2,1)S(1)}, u32[]{:S(2)}, u32[]{:S(2)}) collective-permute-start(bf16[8,48,128]{2,1,0:T(8,128)(2,1)S(1)} %slice.39), channel_id=1, source_target_pairs={{0,2},{1,3},{2,0},{3,1},{4,6},{5,7},{6,4},{7,5},{8,10},{9,11},{10,... | collective-permute-start | bytes 294920 | tf_op jit(solution)/shard_map/ppermute | solution.py:238
  15.2 4.7 %collective-permute-start.2 = (bf16[8,48,128]{2,1,0:T(8,128)(2,1)S(1)}, bf16[8,48,128]{2,1,0:T(8,128)(2,1)S(1)}, u32[]{:S(2)}, u32[]{:S(2)}) collective-permute-start(bf16[8,48,128]{2,1,0:T(8,128)(2,1)S(1)} %fusion.2), channel_id=1, source_target_pairs={{0,4},{1,5},{2,6},{3,7},{4,0},{5,1},{6,2},{7,3},{8,12},{9,13},{10,... | collective-permute-start | bytes 294920 | tf_op jit(solution)/shard_map/ppermute | solution.py:238
  19.9 5.6 %collective-permute-start.3 = (bf16[8,48,128]{2,1,0:T(8,128)(2,1)S(1)}, bf16[8,48,128]{2,1,0:T(8,128)(2,1)S(1)}, u32[]{:S(2)}, u32[]{:S(2)}) collective-permute-start(bf16[8,48,128]{2,1,0:T(8,128)(2,1)S(1)} %fusion), channel_id=1, source_target_pairs={{0,8},{1,9},{2,10},{3,11},{4,12},{5,13},{6,14},{7,15},{8,0},{9,1},... | collective-permute-start | bytes 294920 | tf_op jit(solution)/shard_map/ppermute | solution.py:238
  25.5 5.4 %collective-permute-start.4 = (bf16[8,48,128]{2,1,0:T(8,128)(2,1)S(1)}, bf16[8,48,128]{2,1,0:T(8,128)(2,1)S(1)}, u32[]{:S(2)}, u32[]{:S(2)}) collective-permute-start(bf16[8,48,128]{2,1,0:T(8,128)(2,1)S(1)} %add_convert_fusion.refs_0_), channel_id=1, source_target_pairs={{0,2},{1,3},{2,0},{3,1},{4,6},{5,7},{6,4},{7,5},{8,10},{9,11},{10,... | collective-permute-start | bytes 294920 | tf_op jit(solution)/shard_map/ppermute | solution.py:238
  28.4 2.6 %collective-permute-start.5 = (bf16[8,48,128]{2,1,0:T(8,128)(2,1)S(1)}, bf16[8,48,128]{2,1,0:T(8,128)(2,1)S(1)}, u32[]{:S(2)}, u32[]{:S(2)}) collective-permute-start(bf16[8,48,128]{2,1,0:T(8,128)(2,1)S(1)} %add_convert_fusion.refs_0_), channel_id=1, source_target_pairs={{0,1},{1,0},{2,3},{3,2},{4,5},{5,4},{6,7},{7,6},{8,9},{9,8},{10,11... | collective-permute-start | bytes 294920 | tf_op jit(solution)/shard_map/ppermute | solution.py:238
  31.0 1.3 %collective-permute-start.6 = (bf16[8,48,128]{2,1,0:T(8,128)(2,1)S(1)}, bf16[8,48,128]{2,1,0:T(8,128)(2,1)S(1)}, u32[]{:S(2)}, u32[]{:S(2)}) collective-permute-start(bf16[8,48,128]{2,1,0:T(8,128)(2,1)S(1)} %collective-permute-done.4.refs_1_), channel_id=1, source_target_pairs={{0,1},{1,0},{2,3},{3,2},{4,5},{5,4},{6,7},{7,6},{8,9},{9,8},{10,11... | collective-permute-start | bytes 294920 | tf_op jit(solution)/shard_map/ppermute | solution.py:238
  35.6 1.8 %collective-permute-start.7 = (f32[16,48,128]{2,1,0:T(8,128)S(1)}, f32[16,48,128]{2,1,0:T(8,128)S(1)}, u32[]{:S(2)}, u32[]{:S(2)}) collective-permute-start(f32[16,48,128]{2,1,0:T(8,128)S(1)} %get-tuple-element.11), channel_id=1, source_target_pairs={{0,1},{1,0},{2,3},{3,2},{4,5},{5,4},{6,7},{7,6},{8,9},{9,8},{10,11... | collective-permute-start | bytes 1179656 | tf_op jit(solution)/shard_map/ppermute | solution.py:238
  37.4 5.2 %collective-permute-start.8 = (bf16[8,48,128]{2,1,0:T(8,128)(2,1)S(1)}, bf16[8,48,128]{2,1,0:T(8,128)(2,1)S(1)}, u32[]{:S(2)}, u32[]{:S(2)}) collective-permute-start(bf16[8,48,128]{2,1,0:T(8,128)(2,1)S(1)} %slice.38), channel_id=1, source_target_pairs={{0,2},{1,3},{2,0},{3,1},{4,6},{5,7},{6,4},{7,5},{8,10},{9,11},{10,... | collective-permute-start | bytes 294920 | tf_op jit(solution)/shard_map/ppermute | solution.py:238
  42.6 4.7 %collective-permute-start.9 = (bf16[8,48,128]{2,1,0:T(8,128)(2,1)S(1)}, bf16[8,48,128]{2,1,0:T(8,128)(2,1)S(1)}, u32[]{:S(2)}, u32[]{:S(2)}) collective-permute-start(bf16[8,48,128]{2,1,0:T(8,128)(2,1)S(1)} %fusion.3), channel_id=1, source_target_pairs={{0,4},{1,5},{2,6},{3,7},{4,0},{5,1},{6,2},{7,3},{8,12},{9,13},{10,... | collective-permute-start | bytes 294920 | tf_op jit(solution)/shard_map/ppermute | solution.py:238
  47.3 6.6 %collective-permute-start.10 = (bf16[8,48,128]{2,1,0:T(8,128)(2,1)S(1)}, bf16[8,48,128]{2,1,0:T(8,128)(2,1)S(1)}, u32[]{:S(2)}, u32[]{:S(2)}) collective-permute-start(bf16[8,48,128]{2,1,0:T(8,128)(2,1)S(1)} %fusion.1), channel_id=1, source_target_pairs={{0,8},{1,9},{2,10},{3,11},{4,12},{5,13},{6,14},{7,15},{8,0},{9,1},... | collective-permute-start | bytes 294920 | tf_op jit(solution)/shard_map/ppermute | solution.py:238
  54.0 4.7 %collective-permute-start.11 = (bf16[8,48,128]{2,1,0:T(8,128)(2,1)S(1)}, bf16[8,48,128]{2,1,0:T(8,128)(2,1)S(1)}, u32[]{:S(2)}, u32[]{:S(2)}) collective-permute-start(bf16[8,48,128]{2,1,0:T(8,128)(2,1)S(1)} %get-tuple-element.12.refs_0_), channel_id=1, source_target_pairs={{0,2},{1,3},{2,0},{3,1},{4,6},{5,7},{6,4},{7,5},{8,10},{9,11},{10,... | collective-permute-start | bytes 294920 | tf_op jit(solution)/shard_map/ppermute | solution.py:238
  55.3 3.4 %collective-permute-start.12 = (bf16[8,48,128]{2,1,0:T(8,128)(2,1)S(1)}, bf16[8,48,128]{2,1,0:T(8,128)(2,1)S(1)}, u32[]{:S(2)}, u32[]{:S(2)}) collective-permute-start(bf16[8,48,128]{2,1,0:T(8,128)(2,1)S(1)} %get-tuple-element.12.refs_0_), channel_id=1, source_target_pairs={{0,1},{1,0},{2,3},{3,2},{4,5},{5,4},{6,7},{7,6},{8,9},{9,8},{10,11... | collective-permute-start | bytes 294920 | tf_op jit(solution)/shard_map/ppermute | solution.py:238
  58.7 1.3 %collective-permute-start.13 = (bf16[8,48,128]{2,1,0:T(8,128)(2,1)S(1)}, bf16[8,48,128]{2,1,0:T(8,128)(2,1)S(1)}, u32[]{:S(2)}, u32[]{:S(2)}) collective-permute-start(bf16[8,48,128]{2,1,0:T(8,128)(2,1)S(1)} %collective-permute-done.11.refs_1_), channel_id=1, source_target_pairs={{0,1},{1,0},{2,3},{3,2},{4,5},{5,4},{6,7},{7,6},{8,9},{9,8},{10,11... | collective-permute-start | bytes 294920 | tf_op jit(solution)/shard_map/ppermute | solution.py:238

commit v4 on v3

--- a/solution.py
+++ b/solution.py
@@ -61,6 +61,22 @@
         ok = t + k < live[b]
         rows.append(jnp.where(ok if valid is None else ok & valid, row, dead))
     return slot, b, rows
+
+
+def rounds(total, state, work):
+    whole = lax.shift_right_logical(total, PAIRS.bit_length() - 1)
+    state = lax.fori_loop(0, whole, lambda c, state: work(PAIRS, c * PAIRS, state), state)
+    begin, size = whole * PAIRS, PAIRS // 2
+    while size >= LEAST:
+        left = total - begin
+        if size > LEAST:
+            more = (left >= size).astype(jnp.int32)
+        else:
+            more = lax.div(left + size - 1, size)
+        state = lax.fori_loop(0, more, lambda c, state, begin=begin, size=size: work(size, begin + c * size, state), state)
+        begin = begin + more * size
+        size //= 2
+    return state
 
 
 def chunks(live, screen, slots, total, dead, own, quarter, bits, ready_heads, ready_tails, work):
@@ -88,18 +104,8 @@
         work(entries)
         return waited
 
-    whole = lax.shift_right_logical(total, PAIRS.bit_length() - 1)
-    waited = lax.fori_loop(0, whole, lambda c, waited: tail(PAIRS, c * PAIRS, waited), 0)
-    begin, size = whole * PAIRS, PAIRS // 2
-    while size >= LEAST:
-        left = total - begin
-        if size > LEAST:
-            more = (left >= size).astype(jnp.int32)
-        else:
-            more = lax.div(left + size - 1, size)
-        waited = lax.fori_loop(0, more, lambda c, waited, begin=begin, size=size: tail(size, begin + c * size, waited), waited)
-        begin = begin + more * size
-        size //= 2
+    rounds(total, 0, tail)
+
 
 def gamma_kernel(own, axis, live_h, screen_h, density_h, table_h, near, far, table, live, screen, slots, density, acc, small_sem, head_sem, tail_sem):
     blocks, per_block = screen.shape
@@ -165,93 +171,155 @@
     far[...] = acc[half : 2 * half]
 
 
-def response_kernel(own, axis, live_h, screen_h, table, *refs):
-    coefs, (sums, out, mine, live, screen, slots, coef, acc, small_sem) = refs[:4], refs[4:]
+def plan_size(blocks, per_block):
+    return blocks * per_block + 2 * LEAST + 1
+
+
+def plan_kernel(own, axis, quarter, base, live_h, screen_h, plan, live, screen, sem):
     blocks, per_block = screen.shape
-    quarter, states, aux = coefs[0].shape
-    bits = place(axis)
-    small = [
-        pltpu.make_async_copy(live_h, live, small_sem.at[0]),
-        pltpu.make_async_copy(screen_h, screen, small_sem.at[1]),
-    ]
+    size = plan_size(blocks, per_block)
+    first, second = place(axis)
+    small = [pltpu.make_async_copy(live_h, live, sem.at[0]), pltpu.make_async_copy(screen_h, screen, sem.at[1])]
     for copy in small:
         copy.start()
+    for copy in small:
+        copy.wait()
+    dead = 2 * quarter
+
+    def block(b, counts):
+        def one(t, counts):
+            mine, other = counts
+            owner, rest = divide(screen[b, t], own)
+            side = (lax.shift_right_logical(owner, 1) & 1) ^ second
+            row = ((owner & 1) ^ first) * quarter + lax.shift_right_logical(owner, 2) * own + rest
+            plan[jnp.where(side == 0, mine, size + other)] = (b * per_block + t) * base + row
+            return mine + 1 - side, other + side
+
+        mine, other = lax.fori_loop(0, live[b], one, counts)
+        plan[mine] = b * per_block * base + dead
+        plan[size + other] = b * per_block * base + dead
+        return mine + (mine & 1), other + (other & 1)
+
+    counts = lax.fori_loop(0, blocks, block, (0, 0))
+    for k in (0, 1):
+        for p in range(2 * LEAST):
+            plan[k * size + counts[k] + p] = dead
+        plan[(k + 1) * size - 1] = counts[k]
+
+
+def add_responses(side, per_block, base, plan, table, coefs, coef, acc):
+    quarter, states, aux = coefs[0].shape
+    size = plan.shape[0] // 2
+    for k in (0, 1):
+        coef[k * quarter : (k + 1) * quarter] = coefs[k][...]
+    coef[2 * quarter] = jnp.zeros((states, aux), BF16)
+
+    def work(count, begin, state):
+        products = []
+        for p in range(count):
+            entries = [divide(plan[side * size + 2 * (begin + p) + k], base) for k in (0, 1)]
+            tiles = [table[pl.ds(pl.multiple_of(slot * aux, aux), aux), :] for slot, _ in entries]
+            picked = jnp.concatenate([coef[row] for _, row in entries], axis=1)
+            product = lax.dot_general(picked, jnp.concatenate(tiles, axis=0), NN, preferred_element_type=F32)
+            products.append((divide(entries[0][0], per_block)[0], product))
+        for b, product in products:
+            acc[b] = acc[b] + product
+        return state
+
+    rounds(lax.shift_right_logical(plan[(side + 1) * size - 1], 1), 0, work)
+
+
+def first_response_kernel(per_block, base, plan, table, coef_a, coef_b, acc, coef):
     acc[...] = jnp.zeros_like(acc)
+    add_responses(0, per_block, base, plan, table, (coef_a, coef_b), coef, acc)
+
+
+def second_response_kernel(per_block, base, own, axis, plan, table, coef_a, coef_b, before, sums, out, mine, coef, acc):
     mine[...] = sums[pl.ds(lax.shift_right_logical(lax.axis_index(axis), 2) * own, own)]
-    for k in range(4):
-        coef[k * quarter : (k + 1) * quarter] = coefs[k][...]
-    coef[4 * quarter] = jnp.zeros((states, aux), BF16)
-    small[0].wait()
-    total = list_tails(live, slots, blocks, per_block)
-    small[1].wait()
-
-    def work(entries):
-        products = []
-        for slot, b, rows in entries:
-            tile = table[pl.ds(pl.multiple_of(slot * aux, 2 * aux), 2 * aux), :]
-            picked = jnp.concatenate([coef[rows[0]], coef[rows[1]]], axis=1)
-            products.append(lax.dot_general(picked, tile, NN, preferred_element_type=F32))
-        for (_, b, _), product in zip(entries, products):
-            acc[b] = acc[b] + product
-
-    chunks(live, screen, slots, total, 4 * quarter, own, quarter, bits, lambda b, count: None, lambda begin, end: end, work)
+    acc[...] = before[...]
+    add_responses(1, per_block, base, plan, table, (coef_a, coef_b), coef, acc)
     out[...] = acc[...].astype(out.dtype)
 
 
-def metric_kernel(own, axis, *refs):
-    gammas, (metric, near, far, high, low) = refs[:4], refs[4:]
-    quarter, states, aux = gammas[0].shape
-    rows = metric.shape[0]
-    width = own * aux
+def columns(h, k, width, axis):
     first, second = place(axis)
-
-    def columns(h, k):
-        owner = (h * 2 + ((k & 1) ^ second)) * 2 + ((k >> 1) ^ first)
-        return pl.ds(pl.multiple_of(owner * width, width), width)
-
-    fitted = jnp.zeros((states, rows), F32)
+    owner = (h * 2 + ((k & 1) ^ second)) * 2 + ((k >> 1) ^ first)
+    return pl.ds(pl.multiple_of(owner * width, width), width)
+
+
+def fit(own, axis, sides, gammas, high, low, fitted):
+    quarter, _, aux = gammas[0].shape
     for h in range(quarter // own):
-        for k in range(4):
-            part = columns(h, k)
-            whole = metric[:, part]
-            m_high = whole.astype(BF16)
-            m_low = (whole - m_high.astype(F32)).astype(BF16)
-            high[:, part] = m_high
-            low[:, part] = m_low
-            g = jnp.concatenate([gammas[k][h * own + j] for j in range(own)], axis=1)
-            fitted += lax.dot_general(g, m_high, NT, preferred_element_type=F32)
-            fitted += lax.dot_general(g, m_low, NT, preferred_element_type=F32)
+        for k, gamma in zip(sides, gammas):
+            part = columns(h, k, own * aux, axis)
+            g = jnp.concatenate([gamma[h * own + j] for j in range(own)], axis=1)
+            fitted += lax.dot_general(g, high[:, part], NT, preferred_element_type=F32)
+            fitted += lax.dot_general(g, low[:, part], NT, preferred_element_type=F32)
+    return fitted
+
+
+def spread(own, axis, sides, both, high, low, out):
+    half, states, aux = out.shape
+    for h in range(half // 2 // own):
+        for k in sides:
+            part = columns(h, k, own * aux, axis)
+            c = lax.dot_general(both, high[:, part], NN, preferred_element_type=F32)
+            c = c[:states] + c[states:] + lax.dot_general(both[:states], low[:, part], NN, preferred_element_type=F32)
+            for j in range(own):
+                out[(k & 1) * (half // 2) + h * own + j] = c[:, j * aux : (j + 1) * aux]
+
+
+def first_metric_kernel(own, axis, gamma_a, gamma_b, metric, fitted, high, low):
+    width = own * gamma_a.shape[2]
+    for c in range(metric.shape[1] // width):
+        part = slice(c * width, (c + 1) * width)
+        whole = metric[:, part]
+        m_high = whole.astype(BF16)
+        high[:, part] = m_high
+        low[:, part] = (whole - m_high.astype(F32)).astype(BF16)
+    fitted[...] = fit(own, axis, (0, 2), (gamma_a, gamma_b), high, low, jnp.zeros(fitted.shape, F32))
+
+
+def second_metric_kernel(own, axis, gamma_a, gamma_b, before, high, low, far, both):
+    fitted = fit(own, axis, (1, 3), (gamma_a, gamma_b), high, low, before[...])
     fitted_high = fitted.astype(BF16)
     fitted_low = (fitted - fitted_high.astype(F32)).astype(BF16)
-    both = jnp.concatenate([fitted_high, fitted_low], axis=0)
-    for h in range(quarter // own):
-        for k in range(4):
-            part = columns(h, k)
-            c = lax.dot_general(both, high[:, part], NN, preferred_element_type=F32)
-            c = c[:states] + c[states:] + lax.dot_general(fitted_high, low[:, part], NN, preferred_element_type=F32)
-            out = near if k < 2 else far
-            for j in range(own):
-                out[(k & 1) * quarter + h * own + j] = c[:, j * aux : (j + 1) * aux]
+    both[...] = jnp.concatenate([fitted_high, fitted_low], axis=0)
+    spread(own, axis, (2, 3), both[...], high, low, far)
+
+
+def third_metric_kernel(own, axis, both, high, low, near):
+    spread(own, axis, (0, 1), both[...], high, low, near)
 
 
 def exchange(x, axis, devices, bit):
     return lax.ppermute(x, axis, [(j, j ^ bit) for j in range(devices)])
 
 
-def summed(near, far, axis, devices):
+def summed(near, far, axis, devices, inputs=(), aside=None):
     quarter = near.shape[0] // 2
     total = near + exchange(far, axis, devices, 1)
-    total = total[:quarter] + exchange(total[quarter:].astype(BF16), axis, devices, 2).astype(F32)
+    result = None
+    if aside is None:
+        got = exchange(total[quarter:].astype(BF16), axis, devices, 2)
+    else:
+        total, *inputs = lax.optimization_barrier((total, *inputs))
+        got, result = lax.optimization_barrier((exchange(total[quarter:].astype(BF16), axis, devices, 2), aside(*inputs)))
+    total = total[:quarter] + got.astype(F32)
     bit = 4
     while bit < devices:
         total = total + exchange(total.astype(BF16), axis, devices, bit).astype(F32)
         bit *= 2
-    return total
-
-
-def quarters(mine, axis, devices):
+    return total, result
+
+
+def quarters(mine, axis, devices, aside=None):
     other = exchange(mine, axis, devices, 2)
-    return mine, other, exchange(mine, axis, devices, 1), exchange(other, axis, devices, 1)
+    near = exchange(mine, axis, devices, 1)
+    result = None
+    if aside is not None:
+        other, result = lax.optimization_barrier((other, aside(mine, near)))
+    return (mine, other, near, exchange(other, axis, devices, 1)), result
 
 
 def per_device(devices, density, three_index, live, screen, metric_inverse):
@@ -290,36 +358,79 @@
         cost_estimate=pl.CostEstimate(flops=flops, bytes_accessed=table.size * 2, transcendentals=0),
         name="gamma",
     )(in_hbm(live), in_hbm(screen), in_hbm(density), in_hbm(table))
-    gammas = quarters(summed(near, far, axis, devices).astype(BF16), axis, devices)
-
-    near, far = pl.pallas_call(
-        functools.partial(metric_kernel, own, axis),
-        out_shape=tuple(halves),
+    quarter = half // 2
+    base = 1 << (2 * quarter).bit_length()
+    smem = pl.BlockSpec(memory_space=pltpu.SMEM)
+    make_plan = pl.pallas_call(
+        functools.partial(plan_kernel, own, axis, quarter, base),
+        out_shape=jax.ShapeDtypeStruct((2 * plan_size(blocks, per_block),), jnp.int32),
+        in_specs=[anywhere] * 2,
+        out_specs=smem,
+        scratch_shapes=lists[:2] + [pltpu.SemaphoreType.DMA((2,))],
+        compiler_params=pltpu.CompilerParams(vmem_limit_bytes=MIB),
+        cost_estimate=pl.CostEstimate(flops=0, bytes_accessed=6 * MIB, transcendentals=0),
+        name="plan",
+    )
+    gamma, plan = summed(near, far, axis, devices, (live, screen), make_plan)
+    params = pltpu.CompilerParams(vmem_limit_bytes=16 * MIB)
+    rows = metric_inverse.shape[0]
+    terms = [pltpu.VMEM(metric_inverse.shape, BF16)] * 2
+    cost = pl.CostEstimate(flops=2 * metric_inverse.size * states, bytes_accessed=metric_inverse.size, transcendentals=0)
+    first_metric = pl.pallas_call(
+        functools.partial(first_metric_kernel, own, axis),
+        out_shape=(pltpu.VMEM((states, rows), F32), *terms),
+        in_specs=[vmem] * 3,
+        out_specs=(vmem,) * 3,
+        compiler_params=params,
+        cost_estimate=cost,
+        name="metric_first",
+    )
+    gammas, (before, *terms) = quarters(gamma.astype(BF16), axis, devices, lambda a, b: first_metric(a, b, metric_inverse))
+    terms = [pltpu.with_memory_space_constraint(x, pltpu.VMEM) for x in terms]
+    far, both = pl.pallas_call(
+        functools.partial(second_metric_kernel, own, axis),
+        out_shape=(halves[0], pltpu.VMEM((2 * states, rows), BF16)),
         in_specs=[vmem] * 5,
+        out_specs=(vmem,) * 2,
+        compiler_params=params,
+        cost_estimate=cost,
+        name="metric_second",
+    )(gammas[1], gammas[3], before, *terms)
+    near = pl.pallas_call(
+        functools.partial(third_metric_kernel, own, axis),
+        out_shape=halves[0],
+        in_specs=[vmem] * 3,
+        out_specs=vmem,
+        compiler_params=params,
+        cost_estimate=cost,
+        name="metric_third",
+    )(both, *terms)
+    total, _ = summed(near, far, axis, devices)
+
+    table = pltpu.with_memory_space_constraint(table, pltpu.VMEM)
+    spare = pltpu.VMEM((half + 1, states, aux), BF16)
+    cost = pl.CostEstimate(flops=flops // 2, bytes_accessed=table.size, transcendentals=0)
+    first_response = pl.pallas_call(
+        functools.partial(first_response_kernel, per_block, base),
+        out_shape=pltpu.VMEM(density.shape, F32),
+        in_specs=[smem] + [vmem] * 3,
+        out_specs=vmem,
+        scratch_shapes=[spare],
+        compiler_params=params,
+        cost_estimate=cost,
+        name="response_first",
+    )
+    rounded, before = quarters(total.astype(BF16), axis, devices, lambda a, b: first_response(plan, table, a, b))
+    return pl.pallas_call(
+        functools.partial(second_response_kernel, per_block, base, own, axis),
+        out_shape=(jax.ShapeDtypeStruct(density.shape, BF16), jax.ShapeDtypeStruct((own, states, aux), F32)),
+        in_specs=[smem] + [vmem] * 5,
         out_specs=(vmem, vmem),
-        scratch_shapes=[pltpu.VMEM(metric_inverse.shape, BF16)] * 2,
-        compiler_params=pltpu.CompilerParams(vmem_limit_bytes=24 * MIB),
-        cost_estimate=pl.CostEstimate(flops=10 * metric_inverse.size * states, bytes_accessed=metric_inverse.size * 4, transcendentals=0),
-        name="metric",
-    )(*gammas, metric_inverse)
-    total = summed(near, far, axis, devices)
-    rounded = quarters(total.astype(BF16), axis, devices)
-
-    return pl.pallas_call(
-        functools.partial(response_kernel, own, axis),
-        out_shape=(jax.ShapeDtypeStruct(density.shape, BF16), jax.ShapeDtypeStruct((own, states, aux), F32)),
-        in_specs=[anywhere] * 2 + [vmem] * 6,
-        out_specs=(vmem, vmem),
-        scratch_shapes=lists
-        + [
-            pltpu.VMEM((2 * half + 1, states, aux), BF16),
-            pltpu.VMEM(density.shape, F32),
-            pltpu.SemaphoreType.DMA((2,)),
-        ],
-        compiler_params=pltpu.CompilerParams(vmem_limit_bytes=16 * MIB),
-        cost_estimate=pl.CostEstimate(flops=flops, bytes_accessed=table.size * 2, transcendentals=0),
-        name="response",
-    )(live, screen, pltpu.with_memory_space_constraint(table, pltpu.VMEM), *rounded, total)
+        scratch_shapes=[spare, pltpu.VMEM(density.shape, F32)],
+        compiler_params=params,
+        cost_estimate=cost,
+        name="response_second",
+    )(plan, table, rounded[1], rounded[3], before, total)
 
 
 def solution(mesh):

time: 63.3 us -> 60.8 us (0.961)
  Pallas kernels: 11.8 us -> 17.9 us
  waiting for transfers between devices: 32.3 us -> 27.5 us
  starting transfers between devices: 18 us -> 14.7 us
    pallas_call x2 -> x6, Pallas kernels: 6.47 us -> 11.3 us  [the longest x1 3.34 us: summed(): aside(*inputs)]
    ppermute x14, waiting for transfers between devices: 32.3 us -> 27.5 us  [exchange(): return lax.ppermute(x, axis, [(j, j ^ bit) for j in range(devices)])]
    ppermute x14, starting transfers between devices: 18 us -> 14.7 us  [exchange(): return lax.ppermute(x, axis, [(j, j ^ bit) for j in range(devices)])]
    pallas_call x1, Pallas kernels: 5.34 us -> 6.59 us  [per_device(): pl.pallas_call(functools.partial(gamma_kernel, own, axis), out_shape=(*ha...]
  transfers between devices with their start and end apart: 14 -> 14, of which waited for: 12 -> 13; matrix products, arithmetic and copies ran while one was open for 0% -> 0% of each run, Pallas kernels for 0% -> 12%
where the time goes in v4:
time: 60.8 us; the launch traced here: 61.2 us
  waiting for transfers between devices  27.5 us (45%)
  Pallas kernels  17.9 us (29%)
  starting transfers between devices  14.7 us (24%)
  between operations  0.78 us (1%)
    ppermute x14, waiting for transfers between devices, exchange(): return lax.ppermute(x, axis, [(j, j ^ bit) for j in range(devices)])  27.5 us
    ppermute x14, starting transfers between devices, exchange(): return lax.ppermute(x, axis, [(j, j ^ bit) for j in range(devices)])  14.7 us
    pallas_call x1, Pallas kernels, per_device(): pl.pallas_call(functools.partial(gamma_kernel, own, axis), out_shape=(*ha...  6.59 us
    pallas_call x1, Pallas kernels, summed(): aside(*inputs)  3.34 us
    pallas_call x1, Pallas kernels, per_device(): first_response(plan, table, a, b)  2.32 us
    pallas_call x1, Pallas kernels, per_device(): pl.pallas_call(functools.partial(second_response_kernel, per_block, base,...  2.16 us
    pallas_call x1, Pallas kernels, per_device(): pl.pallas_call(functools.partial(second_metric_kernel, own, axis), out_sh...  1.6 us
    pallas_call x1, Pallas kernels, per_device(): first_metric(a, b, metric_inverse)  1.45 us
  transfers between devices with their start and end apart: 14, of which 13 were waited for; matrix products, arithmetic and copies ran while one was open for 0% of the time, Pallas kernels for 12%

profile of v4, /device:TPU:0, one launch (start us, length us, event | category | flops | bytes accessed | tf_op | source)
XLA Modules:
  0.0 61.2 jit_solution(17330033951647841912)
XLA Ops:
  0.6 0.0 copy-start.1
  0.6 0.0 copy-start.2
  0.7 0.0 copy-start
  0.7 6.6 %gamma.1 = (f32[16,48,128]{2,1,0:T(8,128)S(1)}, f32[16,48,128]{2,1,0:T(8,128)S(1)}, bf16[32768,256]{1,0:T(8,128)(2,1)S(1)}) custom-call(s32[8]{0:T(128)} %live_h.2, s32[8,32]{1,0:T(8,128)} %screen_h.2, bf16[8,48,256]{2,1,0:T(8,128)(2,1)} %density_h.1, bf16[32768,256]{1,0:T(8,128)(2,1)} %bitcast.1), custom_call_target="tpu_custom_call" | custom-call | flops 805306368 | bytes 16777216 | tf_op jit(solution)/shard_map/gamma/pallas_call | solution.py:344
  7.3 0.1 collective-permute-start
  7.3 1.7 %collective-permute-done = f32[16,48,128]{2,1,0:T(8,128)S(1)} collective-permute-done((f32[16,48,128]{2,1,0:T(8,128)S(1)}, f32[16,48,128]{2,1,0:T(8,128)S(1)}, u32[]{:S(2)}, u32[]{:S(2)}) %collective-permute-start) | collective-permute-done | bytes 393248 | tf_op jit(solution)/shard_map/ppermute | solution.py:296
  9.1 1.8 %collective-permute-start.1 = (bf16[8,48,128]{2,1,0:T(8,128)(2,1)S(1)}, bf16[8,48,128]{2,1,0:T(8,128)(2,1)S(1)}, u32[]{:S(2)}, u32[]{:S(2)}) collective-permute-start(bf16[8,48,128]{2,1,0:T(8,128)(2,1)S(1)} %slice.38), channel_id=1, source_target_pairs={{0,2},{1,3},{2,0},{3,1},{4,6},{5,7},{6,4},{7,5},{8,10},{9,11},{10,... | collective-permute-start | bytes 294920 | tf_op jit(solution)/shard_map/ppermute | solution.py:296
  10.9 0.0 copy-done.1
  10.9 0.0 copy-done.2
  10.9 3.3 %plan.1 = s32[546]{0:T(1024)S(1)} custom-call(s32[8]{0:T(128)S(1)} %copy-done.2, s32[8,32]{1,0:T(8,128)S(1)} %copy-done.1), custom_call_target="tpu_custom_call" | custom-call | bytes 6291456 | tf_op jit(solution)/shard_map/plan/pallas_call | solution.py:307
  14.2 0.0 collective-permute-done.1
  14.3 1.6 %collective-permute-start.2 = (bf16[8,48,128]{2,1,0:T(8,128)(2,1)S(1)}, bf16[8,48,128]{2,1,0:T(8,128)(2,1)S(1)}, u32[]{:S(2)}, u32[]{:S(2)}) collective-permute-start(bf16[8,48,128]{2,1,0:T(8,128)(2,1)S(1)} %fusion.2), channel_id=1, source_target_pairs={{0,4},{1,5},{2,6},{3,7},{4,0},{5,1},{6,2},{7,3},{8,12},{9,13},{10,... | collective-permute-start | bytes 294920 | tf_op jit(solution)/shard_map/ppermute | solution.py:296
  15.9 3.1 %collective-permute-done.2 = bf16[8,48,128]{2,1,0:T(8,128)(2,1)S(1)} collective-permute-done((bf16[8,48,128]{2,1,0:T(8,128)(2,1)S(1)}, bf16[8,48,128]{2,1,0:T(8,128)(2,1)S(1)}, u32[]{:S(2)}, u32[]{:S(2)}) %collective-permute-start.2) | collective-permute-done | bytes 98336 | tf_op jit(solution)/shard_map/ppermute | solution.py:296
  19.0 4.8 %collective-permute-start.3 = (bf16[8,48,128]{2,1,0:T(8,128)(2,1)S(1)}, bf16[8,48,128]{2,1,0:T(8,128)(2,1)S(1)}, u32[]{:S(2)}, u32[]{:S(2)}) collective-permute-start(bf16[8,48,128]{2,1,0:T(8,128)(2,1)S(1)} %fusion), channel_id=1, source_target_pairs={{0,8},{1,9},{2,10},{3,11},{4,12},{5,13},{6,14},{7,15},{8,0},{9,1},... | collective-permute-start | bytes 294920 | tf_op jit(solution)/shard_map/ppermute | solution.py:296
  23.8 2.8 %collective-permute-done.3 = bf16[8,48,128]{2,1,0:T(8,128)(2,1)S(1)} collective-permute-done((bf16[8,48,128]{2,1,0:T(8,128)(2,1)S(1)}, bf16[8,48,128]{2,1,0:T(8,128)(2,1)S(1)}, u32[]{:S(2)}, u32[]{:S(2)}) %collective-permute-start.3) | collective-permute-done | bytes 98336 | tf_op jit(solution)/shard_map/ppermute | solution.py:296
  26.7 0.1 collective-permute-start.5
  26.7 0.7 %collective-permute-start.4 = (bf16[8,48,128]{2,1,0:T(8,128)(2,1)S(1)}, bf16[8,48,128]{2,1,0:T(8,128)(2,1)S(1)}, u32[]{:S(2)}, u32[]{:S(2)}) collective-permute-start(bf16[8,48,128]{2,1,0:T(8,128)(2,1)S(1)} %add_convert_fusion.gamma_a), channel_id=1, source_target_pairs={{0,2},{1,3},{2,0},{3,1},{4,6},{5,7},{6,4},{7,5},{8,10},{9,11},{10,... | collective-permute-start | bytes 294920 | tf_op jit(solution)/shard_map/ppermute | solution.py:296
  27.4 0.6 %collective-permute-done.5.gamma_b = bf16[8,48,128]{2,1,0:T(8,128)(2,1)S(1)} collective-permute-done((bf16[8,48,128]{2,1,0:T(8,128)(2,1)S(1)}, bf16[8,48,128]{2,1,0:T(8,128)(2,1)S(1)}, u32[]{:S(2)}, u32[]{:S(2)}) %collective-permute-start.5) | collective-permute-done | bytes 98336 | tf_op jit(solution)/shard_map/ppermute | solution.py:296
  28.0 0.0 copy-done
  28.0 1.5 %metric_first.1 = (f32[48,256]{1,0:T(8,128)S(1)}, bf16[256,4096]{1,0:T(8,128)(2,1)S(1)}, bf16[256,4096]{1,0:T(8,128)(2,1)S(1)}) custom-call(bf16[8,48,128]{2,1,0:T(8,128)(2,1)S(1)} %add_convert_fusion.gamma_a, bf16[8,48,128]{2,1,0:T(8,128)(2,1)S(1)} %collective-permute-done.5.gamma_b, f32[256,4096]{1,0:T(8,128)S(1)} %copy-done), custom_call_target="tpu_custom_call" | custom-call | flops 100663296 | bytes 1048576 | tf_op jit(solution)/shard_map/metric_first/pallas_call | solution.py:388
  29.5 2.5 %collective-permute-done.4.gamma_a = bf16[8,48,128]{2,1,0:T(8,128)(2,1)S(1)} collective-permute-done((bf16[8,48,128]{2,1,0:T(8,128)(2,1)S(1)}, bf16[8,48,128]{2,1,0:T(8,128)(2,1)S(1)}, u32[]{:S(2)}, u32[]{:S(2)}) %collective-permute-start.4) | collective-permute-done | bytes 98336 | tf_op jit(solution)/shard_map/ppermute | solution.py:296
  32.0 0.0 collective-permute-start.6
  32.0 1.3 %collective-permute-done.6.gamma_b = bf16[8,48,128]{2,1,0:T(8,128)(2,1)S(1)} collective-permute-done((bf16[8,48,128]{2,1,0:T(8,128)(2,1)S(1)}, bf16[8,48,128]{2,1,0:T(8,128)(2,1)S(1)}, u32[]{:S(2)}, u32[]{:S(2)}) %collective-permute-start.6) | collective-permute-done | bytes 98336 | tf_op jit(solution)/shard_map/ppermute | solution.py:296
  33.3 1.6 %metric_second.1 = (f32[16,48,128]{2,1,0:T(8,128)S(1)}, bf16[96,256]{1,0:T(8,128)(2,1)S(1)}) custom-call(bf16[8,48,128]{2,1,0:T(8,128)(2,1)S(1)} %collective-permute-done.4.gamma_a, bf16[8,48,128]{2,1,0:T(8,128)(2,1)S(1)} %collective-permute-done.6.gamma_b, f32[48,256]{1,0:T(8,128)S(1)} %get-tuple-element.33.before, ...), custom_call_target="tpu_custom_call" | custom-call | flops 100663296 | bytes 1048576 | tf_op jit(solution)/shard_map/metric_second/pallas_call | solution.py:390
  34.9 0.2 collective-permute-start.7
  35.0 0.5 metric_third.1
  35.5 1.1 %collective-permute-done.7 = f32[16,48,128]{2,1,0:T(8,128)S(1)} collective-permute-done((f32[16,48,128]{2,1,0:T(8,128)S(1)}, f32[16,48,128]{2,1,0:T(8,128)S(1)}, u32[]{:S(2)}, u32[]{:S(2)}) %collective-permute-start.7) | collective-permute-done | bytes 393248 | tf_op jit(solution)/shard_map/ppermute | solution.py:296
  36.7 0.7 %collective-permute-start.8 = (bf16[8,48,128]{2,1,0:T(8,128)(2,1)S(1)}, bf16[8,48,128]{2,1,0:T(8,128)(2,1)S(1)}, u32[]{:S(2)}, u32[]{:S(2)}) collective-permute-start(bf16[8,48,128]{2,1,0:T(8,128)(2,1)S(1)} %slice.37), channel_id=1, source_target_pairs={{0,2},{1,3},{2,0},{3,1},{4,6},{5,7},{6,4},{7,5},{8,10},{9,11},{10,... | collective-permute-start | bytes 294920 | tf_op jit(solution)/shard_map/ppermute | solution.py:296
  37.4 4.2 %collective-permute-done.8 = bf16[8,48,128]{2,1,0:T(8,128)(2,1)S(1)} collective-permute-done((bf16[8,48,128]{2,1,0:T(8,128)(2,1)S(1)}, bf16[8,48,128]{2,1,0:T(8,128)(2,1)S(1)}, u32[]{:S(2)}, u32[]{:S(2)}) %collective-permute-start.8) | collective-permute-done | bytes 98336 | tf_op jit(solution)/shard_map/ppermute | solution.py:296
  41.6 0.1 collective-permute-start.9
  41.7 4.6 %collective-permute-done.9 = bf16[8,48,128]{2,1,0:T(8,128)(2,1)S(1)} collective-permute-done((bf16[8,48,128]{2,1,0:T(8,128)(2,1)S(1)}, bf16[8,48,128]{2,1,0:T(8,128)(2,1)S(1)}, u32[]{:S(2)}, u32[]{:S(2)}) %collective-permute-start.9) | collective-permute-done | bytes 98336 | tf_op jit(solution)/shard_map/ppermute | solution.py:296
  46.3 3.4 %collective-permute-start.10 = (bf16[8,48,128]{2,1,0:T(8,128)(2,1)S(1)}, bf16[8,48,128]{2,1,0:T(8,128)(2,1)S(1)}, u32[]{:S(2)}, u32[]{:S(2)}) collective-permute-start(bf16[8,48,128]{2,1,0:T(8,128)(2,1)S(1)} %fusion.1), channel_id=1, source_target_pairs={{0,8},{1,9},{2,10},{3,11},{4,12},{5,13},{6,14},{7,15},{8,0},{9,1},... | collective-permute-start | bytes 294920 | tf_op jit(solution)/shard_map/ppermute | solution.py:296
  49.8 2.6 %collective-permute-done.10 = bf16[8,48,128]{2,1,0:T(8,128)(2,1)S(1)} collective-permute-done((bf16[8,48,128]{2,1,0:T(8,128)(2,1)S(1)}, bf16[8,48,128]{2,1,0:T(8,128)(2,1)S(1)}, u32[]{:S(2)}, u32[]{:S(2)}) %collective-permute-start.10) | collective-permute-done | bytes 98336 | tf_op jit(solution)/shard_map/ppermute | solution.py:296
  52.5 0.1 collective-permute-start.12
  52.6 1.2 %collective-permute-start.11 = (bf16[8,48,128]{2,1,0:T(8,128)(2,1)S(1)}, bf16[8,48,128]{2,1,0:T(8,128)(2,1)S(1)}, u32[]{:S(2)}, u32[]{:S(2)}) collective-permute-start(bf16[8,48,128]{2,1,0:T(8,128)(2,1)S(1)} %get-tuple-element.40.coef_a), channel_id=1, source_target_pairs={{0,2},{1,3},{2,0},{3,1},{4,6},{5,7},{6,4},{7,5},{8,10},{9,11},{10,... | collective-permute-start | bytes 294920 | tf_op jit(solution)/shard_map/ppermute | solution.py:296
  53.8 0.1 collective-permute-done.12.coef_b
  53.8 2.3 %response_first.1.before = f32[8,48,256]{2,1,0:T(8,128)S(1)} custom-call(s32[546]{0:T(1024)S(1)} %plan.1, bf16[32768,256]{1,0:T(8,128)(2,1)S(1)} %get-tuple-element.27.table, bf16[8,48,128]{2,1,0:T(8,128)(2,1)S(1)} %get-tuple-element.40.coef_a, bf16[8,48,128]{2,1,0:T(8,128)(2,1)S(1)} %collective-permute-done.12.coef_b), custom_call_target="tpu_custom_call" | custom-call | flops 402653184 | bytes 8388608 | tf_op jit(solution)/shard_map/response_first/pallas_call | solution.py:423
  56.2 1.6 %collective-permute-done.11.coef_a = bf16[8,48,128]{2,1,0:T(8,128)(2,1)S(1)} collective-permute-done((bf16[8,48,128]{2,1,0:T(8,128)(2,1)S(1)}, bf16[8,48,128]{2,1,0:T(8,128)(2,1)S(1)}, u32[]{:S(2)}, u32[]{:S(2)}) %collective-permute-start.11) | collective-permute-done | bytes 98336 | tf_op jit(solution)/shard_map/ppermute | solution.py:296
  57.8 0.0 collective-permute-start.13
  57.8 1.3 %collective-permute-done.13.coef_b = bf16[8,48,128]{2,1,0:T(8,128)(2,1)S(1)} collective-permute-done((bf16[8,48,128]{2,1,0:T(8,128)(2,1)S(1)}, bf16[8,48,128]{2,1,0:T(8,128)(2,1)S(1)}, u32[]{:S(2)}, u32[]{:S(2)}) %collective-permute-start.13) | collective-permute-done | bytes 98336 | tf_op jit(solution)/shard_map/ppermute | solution.py:296
  59.1 2.2 %response_second.1 = (bf16[8,48,256]{2,1,0:T(8,128)(2,1)}, f32[2,48,128]{2,1,0:T(8,128)}) custom-call(s32[546]{0:T(1024)S(1)} %plan.1, bf16[32768,256]{1,0:T(8,128)(2,1)S(1)} %get-tuple-element.27.table, bf16[8,48,128]{2,1,0:T(8,128)(2,1)S(1)} %collective-permute-done.11.coef_a, bf16[8,48,128]{2,1,0:T(8,128)(2,1)S(1)} %collective-permute-done.13.coef_b, ...), custom_call_target="tpu_custom_call" | custom-call | flops 402653184 | bytes 8388608 | tf_op jit(solution)/shard_map/response_second/pallas_call | solution.py:424
  (10 shorter events, 0.3 us)
Async XLA Ops:
  0.6 10.3 %copy-start.1 = (s32[8,32]{1,0:T(8,128)S(1)}, s32[8,32]{1,0:T(8,128)}, u32[]{:S(2)}) copy-start(s32[8,32]{1,0:T(8,128)} %screen_h.2) | copy-start | bytes 3076
  0.6 10.3 %copy-start.2 = (s32[8]{0:T(128)S(1)}, s32[8]{0:T(128)}, u32[]{:S(2)}) copy-start(s32[8]{0:T(128)} %live_h.2) | copy-start | bytes 100
  0.7 27.4 %copy-start = (f32[256,4096]{1,0:T(8,128)S(1)}, f32[256,4096]{1,0:T(8,128)}, u32[]{:S(2)}) copy-start(f32[256,4096]{1,0:T(8,128)} %metric.1) | copy-start | bytes 12582916
  7.3 1.8 %collective-permute-start = (f32[16,48,128]{2,1,0:T(8,128)S(1)}, f32[16,48,128]{2,1,0:T(8,128)S(1)}, u32[]{:S(2)}, u32[]{:S(2)}) collective-permute-start(f32[16,48,128]{2,1,0:T(8,128)S(1)} %get-tuple-element.22), channel_id=1, source_target_pairs={{0,1},{1,0},{2,3},{3,2},{4,5},{5,4},{6,7},{7,6},{8,9},{9,8},{10,11... | collective-permute-start | bytes 1179656 | tf_op jit(solution)/shard_map/ppermute | solution.py:296
  9.1 5.1 %collective-permute-start.1 = (bf16[8,48,128]{2,1,0:T(8,128)(2,1)S(1)}, bf16[8,48,128]{2,1,0:T(8,128)(2,1)S(1)}, u32[]{:S(2)}, u32[]{:S(2)}) collective-permute-start(bf16[8,48,128]{2,1,0:T(8,128)(2,1)S(1)} %slice.38), channel_id=1, source_target_pairs={{0,2},{1,3},{2,0},{3,1},{4,6},{5,7},{6,4},{7,5},{8,10},{9,11},{10,... | collective-permute-start | bytes 294920 | tf_op jit(solution)/shard_map/ppermute | solution.py:296
  14.3 4.7 %collective-permute-start.2 = (bf16[8,48,128]{2,1,0:T(8,128)(2,1)S(1)}, bf16[8,48,128]{2,1,0:T(8,128)(2,1)S(1)}, u32[]{:S(2)}, u32[]{:S(2)}) collective-permute-start(bf16[8,48,128]{2,1,0:T(8,128)(2,1)S(1)} %fusion.2), channel_id=1, source_target_pairs={{0,4},{1,5},{2,6},{3,7},{4,0},{5,1},{6,2},{7,3},{8,12},{9,13},{10,... | collective-permute-start | bytes 294920 | tf_op jit(solution)/shard_map/ppermute | solution.py:296
  19.0 7.6 %collective-permute-start.3 = (bf16[8,48,128]{2,1,0:T(8,128)(2,1)S(1)}, bf16[8,48,128]{2,1,0:T(8,128)(2,1)S(1)}, u32[]{:S(2)}, u32[]{:S(2)}) collective-permute-start(bf16[8,48,128]{2,1,0:T(8,128)(2,1)S(1)} %fusion), channel_id=1, source_target_pairs={{0,8},{1,9},{2,10},{3,11},{4,12},{5,13},{6,14},{7,15},{8,0},{9,1},... | collective-permute-start | bytes 294920 | tf_op jit(solution)/shard_map/ppermute | solution.py:296
  26.7 1.4 %collective-permute-start.5 = (bf16[8,48,128]{2,1,0:T(8,128)(2,1)S(1)}, bf16[8,48,128]{2,1,0:T(8,128)(2,1)S(1)}, u32[]{:S(2)}, u32[]{:S(2)}) collective-permute-start(bf16[8,48,128]{2,1,0:T(8,128)(2,1)S(1)} %add_convert_fusion.gamma_a), channel_id=1, source_target_pairs={{0,1},{1,0},{2,3},{3,2},{4,5},{5,4},{6,7},{7,6},{8,9},{9,8},{10,11... | collective-permute-start | bytes 294920 | tf_op jit(solution)/shard_map/ppermute | solution.py:296
  26.7 5.2 %collective-permute-start.4 = (bf16[8,48,128]{2,1,0:T(8,128)(2,1)S(1)}, bf16[8,48,128]{2,1,0:T(8,128)(2,1)S(1)}, u32[]{:S(2)}, u32[]{:S(2)}) collective-permute-start(bf16[8,48,128]{2,1,0:T(8,128)(2,1)S(1)} %add_convert_fusion.gamma_a), channel_id=1, source_target_pairs={{0,2},{1,3},{2,0},{3,1},{4,6},{5,7},{6,4},{7,5},{8,10},{9,11},{10,... | collective-permute-start | bytes 294920 | tf_op jit(solution)/shard_map/ppermute | solution.py:296
  32.0 1.3 %collective-permute-start.6 = (bf16[8,48,128]{2,1,0:T(8,128)(2,1)S(1)}, bf16[8,48,128]{2,1,0:T(8,128)(2,1)S(1)}, u32[]{:S(2)}, u32[]{:S(2)}) collective-permute-start(bf16[8,48,128]{2,1,0:T(8,128)(2,1)S(1)} %collective-permute-done.4.gamma_a), channel_id=1, source_target_pairs={{0,1},{1,0},{2,3},{3,2},{4,5},{5,4},{6,7},{7,6},{8,9},{9,8},{10,11... | collective-permute-start | bytes 294920 | tf_op jit(solution)/shard_map/ppermute | solution.py:296
  34.9 1.8 %collective-permute-start.7 = (f32[16,48,128]{2,1,0:T(8,128)S(1)}, f32[16,48,128]{2,1,0:T(8,128)S(1)}, u32[]{:S(2)}, u32[]{:S(2)}) collective-permute-start(f32[16,48,128]{2,1,0:T(8,128)S(1)} %get-tuple-element.37), channel_id=1, source_target_pairs={{0,1},{1,0},{2,3},{3,2},{4,5},{5,4},{6,7},{7,6},{8,9},{9,8},{10,11... | collective-permute-start | bytes 1179656 | tf_op jit(solution)/shard_map/ppermute | solution.py:296
  36.7 4.9 %collective-permute-start.8 = (bf16[8,48,128]{2,1,0:T(8,128)(2,1)S(1)}, bf16[8,48,128]{2,1,0:T(8,128)(2,1)S(1)}, u32[]{:S(2)}, u32[]{:S(2)}) collective-permute-start(bf16[8,48,128]{2,1,0:T(8,128)(2,1)S(1)} %slice.37), channel_id=1, source_target_pairs={{0,2},{1,3},{2,0},{3,1},{4,6},{5,7},{6,4},{7,5},{8,10},{9,11},{10,... | collective-permute-start | bytes 294920 | tf_op jit(solution)/shard_map/ppermute | solution.py:296
  41.6 4.7 %collective-permute-start.9 = (bf16[8,48,128]{2,1,0:T(8,128)(2,1)S(1)}, bf16[8,48,128]{2,1,0:T(8,128)(2,1)S(1)}, u32[]{:S(2)}, u32[]{:S(2)}) collective-permute-start(bf16[8,48,128]{2,1,0:T(8,128)(2,1)S(1)} %fusion.3), channel_id=1, source_target_pairs={{0,4},{1,5},{2,6},{3,7},{4,0},{5,1},{6,2},{7,3},{8,12},{9,13},{10,... | collective-permute-start | bytes 294920 | tf_op jit(solution)/shard_map/ppermute | solution.py:296
  46.3 6.1 %collective-permute-start.10 = (bf16[8,48,128]{2,1,0:T(8,128)(2,1)S(1)}, bf16[8,48,128]{2,1,0:T(8,128)(2,1)S(1)}, u32[]{:S(2)}, u32[]{:S(2)}) collective-permute-start(bf16[8,48,128]{2,1,0:T(8,128)(2,1)S(1)} %fusion.1), channel_id=1, source_target_pairs={{0,8},{1,9},{2,10},{3,11},{4,12},{5,13},{6,14},{7,15},{8,0},{9,1},... | collective-permute-start | bytes 294920 | tf_op jit(solution)/shard_map/ppermute | solution.py:296
  52.5 1.4 %collective-permute-start.12 = (bf16[8,48,128]{2,1,0:T(8,128)(2,1)S(1)}, bf16[8,48,128]{2,1,0:T(8,128)(2,1)S(1)}, u32[]{:S(2)}, u32[]{:S(2)}) collective-permute-start(bf16[8,48,128]{2,1,0:T(8,128)(2,1)S(1)} %get-tuple-element.40.coef_a), channel_id=1, source_target_pairs={{0,1},{1,0},{2,3},{3,2},{4,5},{5,4},{6,7},{7,6},{8,9},{9,8},{10,11... | collective-permute-start | bytes 294920 | tf_op jit(solution)/shard_map/ppermute | solution.py:296
  52.6 5.2 %collective-permute-start.11 = (bf16[8,48,128]{2,1,0:T(8,128)(2,1)S(1)}, bf16[8,48,128]{2,1,0:T(8,128)(2,1)S(1)}, u32[]{:S(2)}, u32[]{:S(2)}) collective-permute-start(bf16[8,48,128]{2,1,0:T(8,128)(2,1)S(1)} %get-tuple-element.40.coef_a), channel_id=1, source_target_pairs={{0,2},{1,3},{2,0},{3,1},{4,6},{5,7},{6,4},{7,5},{8,10},{9,11},{10,... | collective-permute-start | bytes 294920 | tf_op jit(solution)/shard_map/ppermute | solution.py:296
  57.8 1.3 %collective-permute-start.13 = (bf16[8,48,128]{2,1,0:T(8,128)(2,1)S(1)}, bf16[8,48,128]{2,1,0:T(8,128)(2,1)S(1)}, u32[]{:S(2)}, u32[]{:S(2)}) collective-permute-start(bf16[8,48,128]{2,1,0:T(8,128)(2,1)S(1)} %collective-permute-done.11.coef_a), channel_id=1, source_target_pairs={{0,1},{1,0},{2,3},{3,2},{4,5},{5,4},{6,7},{7,6},{8,9},{9,8},{10,11... | collective-permute-start | bytes 294920 | tf_op jit(solution)/shard_map/ppermute | solution.py:296
